TPU v7x, 256 devices: a whole 4x4x8 slice. The times are simulated.
256 devices in a mesh: prefix: 32 (over z, y), samples: 8 (over x, core).
Axes of the slice: x: 4, y: 4, z: 8, core: 2. Of those that a mesh axis runs over, the one named last changes fastest.
Arguments:
- query: bfloat16 [256, 8192], P(('samples', 'prefix')), may hold values from -192 to 192
- prompt_code_cache: bfloat16 [2, 65536, 8, 128], P(None, 'prefix'), may hold values from -127 to 127
- prompt_scale_cache: bfloat16 [2, 1024, 8], P(None, 'prefix'), may hold values from 0.00390625 to 0.015625, as said below
- prefix_len: int32 [1], replicated, may hold values from 32768 to 65536
- sample_key_value_cache: bfloat16 [256, 2, 512, 1024], P(('samples', 'prefix')), may hold values from -9 to 9
- suffix_len: int32 [256], P(('samples', 'prefix')), may hold values from 1 to 512, 65536 in all
- w_out: bfloat16 [8192, 8192], P('prefix', 'samples'), may hold values from -0.0625 to 0.0625
Outputs:
- mixed: bfloat16 [256, 8192], P('prefix', 'samples')
Inputs may be any that keep to these rules, and one draw needn't show every extreme that they name: `prompt_scale_cache`: each scale is 2 ** -8, 2 ** -7 or 2 ** -6. `suffix_len`: some sample uses all 512 positions.
All inputs are finite; a program needn't handle non-finite values. No bound on the sum of `suffix_len` on one device may be relied on, other than what follows from the above.
Results may differ from a plain program's by a relative error of at most 0.0075.
Values may be sent and summed in bfloat16 or wider, within the bound.
No kernel may reach another device: no remote copies, remote signals or barrier semaphores. Data moves between devices by JAX's collectives and lax.ppermute only.
A program may use at most 192 MiB of HBM per device.

v0:
```python
import math

import jax
import jax.numpy as jnp
from jax import lax
from jax.sharding import PartitionSpec as P


def attend_block(query_rows, key_rows, value_rows, valid, scale):
    scores = (
        jnp.einsum("sjgd,tjd->sjgt", query_rows, key_rows, preferred_element_type=jnp.float32)
        * scale
    )
    scores = jnp.where(valid, scores, -jnp.inf)
    top = jnp.max(scores, axis=-1)
    safe = jnp.where(top == -jnp.inf, 0.0, top)
    weights = jnp.exp(scores - safe[..., None]).astype(jnp.bfloat16)
    total = jnp.sum(weights, axis=-1, dtype=jnp.float32)
    out = jnp.einsum("sjgt,tjd->sjgd", weights, value_rows, preferred_element_type=jnp.float32)
    return (out, top, total)


def join_partials(first, second):
    out_a, top_a, total_a = first
    out_b, top_b, total_b = second
    top = jnp.maximum(top_a, top_b)
    safe = jnp.where(top == -jnp.inf, 0.0, top)
    factor_a = jnp.exp(top_a - safe)
    factor_b = jnp.exp(top_b - safe)
    return (
        out_a * factor_a[..., None] + out_b * factor_b[..., None],
        top,
        total_a * factor_a + total_b * factor_b,
    )


def body(
    query,
    prompt_code_cache,
    prompt_scale_cache,
    prefix_len,
    sample_key_value_cache,
    suffix_len,
    w_out,
):
    key_value_heads = prompt_code_cache.shape[2]
    head_width = prompt_code_cache.shape[3]
    head_count = query.shape[1] // head_width
    query_group = head_count // key_value_heads
    row_count = prompt_code_cache.shape[1]
    block_count = prompt_scale_cache.shape[1]
    model_width = row_count // block_count
    scale = 1.0 / math.sqrt(head_width)
    my_index = lax.axis_index("prefix")
    collected_rows = lax.all_gather(query, "prefix", axis=0, tiled=True)
    group_members = collected_rows.shape[0]
    grouped_query = collected_rows.reshape(group_members, key_value_heads, query_group, head_width)
    matrix_product = (
        prompt_code_cache.astype(jnp.float32).reshape(
            2, block_count, model_width, key_value_heads, head_width
        )
        * prompt_scale_cache.astype(jnp.float32)[:, :, None, :, None]
    )
    restored_cache = matrix_product.astype(jnp.bfloat16).reshape(
        2, row_count, key_value_heads, head_width
    )
    positions = my_index * row_count + jnp.arange(row_count, dtype=jnp.int32)
    valid = (positions < prefix_len[0])[None, None, None, :]
    block_out, block_top, block_total = attend_block(
        grouped_query, restored_cache[0], restored_cache[1], valid, scale
    )
    sample_query = query.reshape(1, key_value_heads, query_group, head_width)
    continue_max = sample_key_value_cache.shape[2]
    sample_key_rows = sample_key_value_cache[0, 0].reshape(
        continue_max, key_value_heads, head_width
    )
    sample_value_rows = sample_key_value_cache[0, 1].reshape(
        continue_max, key_value_heads, head_width
    )
    own_valid = (jnp.arange(continue_max, dtype=jnp.int32) < suffix_len[0])[None, None, None, :]
    suffix_part = attend_block(sample_query, sample_key_rows, sample_value_rows, own_valid, scale)
    got_out, got_top, got_total = (
        lax.all_to_all(block_out, "prefix", split_axis=0, concat_axis=0, tiled=True),
        lax.all_to_all(block_top, "prefix", split_axis=0, concat_axis=0, tiled=True),
        lax.all_to_all(block_total, "prefix", split_axis=0, concat_axis=0, tiled=True),
    )
    top = jnp.max(got_top, axis=0, keepdims=True)
    safe = jnp.where(top == -jnp.inf, 0.0, top)
    factor = jnp.exp(got_top - safe)
    prompt_part = (
        jnp.sum(got_out * factor[..., None], axis=0, keepdims=True),
        top,
        jnp.sum(got_total * factor, axis=0, keepdims=True),
    )
    numer, top, denom = join_partials(prompt_part, suffix_part)
    attention = (numer / denom[..., None]).astype(jnp.bfloat16).reshape(1, head_count * head_width)
    regrouped = lax.all_to_all(attention, "prefix", split_axis=1, concat_axis=0, tiled=True)
    all_rows = lax.all_gather(regrouped, "samples", axis=0, tiled=True)
    return lax.psum_scatter(
        jnp.dot(all_rows, w_out, preferred_element_type=jnp.float32),
        "prefix",
        scatter_dimension=0,
        tiled=True,
    ).astype(jnp.bfloat16)


def solution(mesh):
    in_specs = (
        P(("samples", "prefix"), None),
        P(None, "prefix", None, None),
        P(None, "prefix", None),
        P(),
        P(("samples", "prefix"), None, None, None),
        P(("samples", "prefix")),
        P("prefix", "samples"),
    )
    out_specs = P("prefix", "samples")
    return jax.shard_map(body, mesh=mesh, in_specs=in_specs, out_specs=out_specs, check_vma=False)
```

profile of v0, /device:TPU:32, one launch (start us, length us, event | category | flops | bytes accessed | tf_op | source)
XLA Modules:
  0.0 410.5 jit_solution(7986097079576190276)
XLA Ops:
  6.5 0.0 copy-start
  6.5 0.0 copy-start.3
  7.3 11.3 %convert.1 = f32[2,32,64,8,128]{4,3,2,1,0:T(8,128)} convert(bf16[2,32,64,8,128]{4,3,2,1,0:T(8,128)(2,1)} %bitcast.89) | non-fusion elementwise | flops 4194304 | bytes 25165824 | tf_op jit(solution)/shard_map/reshape | solution.py:59
  18.6 0.0 copy-done.3
  18.6 0.0 copy-start.2
  18.6 9.6 %fusion.2 = bf16[2,32,64,8,128]{4,2,1,3,0:T(8,128)(2,1)S(1)} fusion(f32[2,32,64,8,128]{4,3,2,1,0:T(8,128)} %convert.1, f32[2,32,8]{1,2,0:T(8,128)S(1)} %convert_element_type.25), kind=kLoop, calls=%fused_computation.5 | loop fusion | flops 8388608 | bytes 25167872 | tf_op jit(solution)/shard_map/convert_element_type | solution.py:64
  28.1 4.2 %fusion.20 = (bf16[1,32,64,8,128]{4,2,1,3,0:T(8,128)(2,1)}, bf16[1,32,64,8,128]{4,2,1,3,0:T(8,128)(2,1)}) fusion(bf16[2,32,64,8,128]{4,2,1,3,0:T(8,128)(2,1)S(1)} %fusion.2), kind=kLoop, calls=%fused_computation.42 | loop fusion | bytes 16777216 | tf_op jit(solution)/shard_map/slice | solution.py:70
  32.4 0.0 copy-done.2
  32.4 52.4 %all-gather.1 = bf16[32,1,8192]{2,1,0:T(2,128)(2,1)S(1)} all-gather(bf16[1,1,8192]{2,1,0:T(2,128)(2,1)S(1)} %bitcast.95), channel_id=1, replica_groups=mesh['prefix'=32,'samples'=8] {'prefix'}, dimensions={0}, use_global_device_ids=true | all-gather | bytes 540672 | tf_op jit(solution)/shard_map/all_gather | solution.py:55
  84.8 3.2 reduce.2
  88.0 0.1 copy.51
  88.2 4.5 %bitcast_reduce_fusion = (f32[32,8,8]{0,2,1:T(8,128)S(1)}, f32[8,2048,32,8]{1,2,3,0:T(8,128)S(1)}) fusion(pred[2048]{0:T(1024)(128)(4,1)S(1)} %add_compare_fusion, bf16[2048,8,128,1]{2,0,3,1:T(8,128)(2,1)} %bitcast.88, bf16[32,8,8,128]{3,2,1,0:T(8,128)(2,1)S(1)} %bitcast.93), kind=kOutput, calls=%fused_computation.1 | convolution fusion | flops 1086322688 | bytes 21506048 | tf_op jit(solution)/shard_map/sjgd,tjd->sjgt/dot_general | solution.py:11
  92.7 0.0 copy-start.1
  92.7 5.7 %copy-done.1 = f32[8,2048,32,8]{1,2,3,0:T(8,128)} copy-done((f32[8,2048,32,8]{1,2,3,0:T(8,128)}, f32[8,2048,32,8]{1,2,3,0:T(8,128)S(1)}, u32[]{:S(2)}) %copy-start.1) | copy-done | bytes 16777240
  98.4 3.8 convert_reduce_fusion
  102.2 0.7 copy.42
  102.9 6.9 %all-to-all-start.2 = ((f32[32,8,8]{2,1,0:T(8,128)}), f32[32,8,8]{2,1,0:T(8,128)S(1)}, u32[]{:S(2)}, u32[]{:S(2)}) async-start(f32[32,8,8]{2,1,0:T(8,128)} %copy.42), calls=%async_computation.2 | async-start | bytes 262144 | tf_op jit(solution)/shard_map/all_to_all | solution.py:85
  109.8 0.7 copy.37
  110.6 9.5 %all-to-all-done.2 = f32[32,8,8]{2,1,0:T(8,128)S(1)} async-done(((f32[32,8,8]{2,1,0:T(8,128)}), f32[32,8,8]{2,1,0:T(8,128)S(1)}, u32[]{:S(2)}, u32[]{:S(2)}) %all-to-all-start.2) | async-done | bytes 8224 | tf_op jit(solution)/shard_map/all_to_all | solution.py:85
  120.0 4.7 %all-to-all-start.1 = ((f32[32,8,8]{2,1,0:T(8,128)}), f32[32,8,8]{2,1,0:T(8,128)S(1)}, u32[]{:S(2)}, u32[]{:S(2)}) async-start(f32[32,8,8]{2,1,0:T(8,128)} %copy.37), calls=%async_computation.1 | async-start | bytes 262144 | tf_op jit(solution)/shard_map/all_to_all | solution.py:84
  124.7 9.1 %convolution_bitcast_fusion = f32[32,8,8,128]{3,0,2,1:T(8,128)S(1)} fusion(bf16[2048,8,128,1]{2,0,3,1:T(8,128)(2,1)} %bitcast.92, f32[8,2048,32,8]{1,2,3,0:T(8,128)} %copy-done.1, f32[32,8,8]{0,2,1:T(8,128)S(1)} %compare_select_fusion, pred[2048]{0:T(1024)(128)(4,1)S(1)} %add_compare_fusion), kind=kOutput, calls=%fused_computation.8 | convolution fusion | flops 1090519040 | bytes 22030336 | tf_op jit(solution)/shard_map/sjgt,tjd->sjgd/dot_general | solution.py:19
  133.9 1.6 copy.36
  135.5 0.0 all-to-all-done.1
  135.5 9.8 %all-to-all-start = ((f32[32,8,8,128]{3,2,1,0:T(8,128)}), f32[32,8,8,128]{3,2,1,0:T(8,128)S(1)}, u32[]{:S(2)}, u32[]{:S(2)}) async-start(f32[32,8,8,128]{3,2,1,0:T(8,128)} %copy.36), calls=%async_computation | async-start | bytes 2097152 | tf_op jit(solution)/shard_map/all_to_all | solution.py:83
  145.3 0.0 reduce-scatter.2.cloned.1.call-start
  145.3 0.1 reduce.3
  145.4 2.7 fusion.21
  148.1 1.3 copy.49
  150.1 1.5 copy.50
  151.7 1.6 fusion.22
  153.2 0.2 convert_reduce_fusion.1
  153.5 9.7 %all-to-all-done = f32[32,8,8,128]{3,2,1,0:T(8,128)S(1)} async-done(((f32[32,8,8,128]{3,2,1,0:T(8,128)}), f32[32,8,8,128]{3,2,1,0:T(8,128)S(1)}, u32[]{:S(2)}, u32[]{:S(2)}) %all-to-all-start) | async-done | bytes 1048608 | tf_op jit(solution)/shard_map/all_to_all | solution.py:83
  163.2 0.3 multiply_reduce_fusion
  163.5 0.4 fusion.10
  164.0 0.5 broadcast.110
  164.5 0.7 reduce.4
  165.2 14.4 %all_to_all.32 = bf16[32,2,128]{2,1,0:T(2,128)(2,1)S(1)} all-to-all(bf16[32,2,128]{2,1,0:T(2,128)(2,1)S(1)} %reshape.146), channel_id=1, replica_groups=mesh['prefix'=32,'samples'=8] {'prefix'}, dimensions={0} | all-to-all | bytes 32768 | tf_op jit(solution)/shard_map/all_to_all | solution.py:97
  179.7 13.1 %all-gather = bf16[1,256,256]{2,1,0:T(8,128)(2,1)S(1)} all-gather(bf16[1,32,256]{2,1,0:T(8,128)(2,1)S(1)} %copy.44), channel_id=2, replica_groups=mesh['prefix'=32,'samples'=8] {'samples'}, dimensions={1}, use_global_device_ids=true | all-gather | bytes 147456 | tf_op jit(solution)/shard_map/all_gather | solution.py:98
  192.8 0.0 copy-done
  192.8 1.3 fusion.14
  194.1 0.0 reduce-scatter.2.cloned.1.call-update
  194.1 208.2 %reduce-scatter.2.cloned.1.call-done = f32[8,1024]{1,0:T(8,128)} async-done(((f32[256,1024]{1,0:T(8,128)}), f32[8,1024]{1,0:T(8,128)}) %reduce-scatter.2.cloned.1.call-update) | async-done | bytes 32784 | tf_op jit(solution)/shard_map/reduce_scatter | solution.py:99
  402.3 1.4 convert_element_type.32
  (13 shorter events, 0.2 us)
Async XLA Ops:
  6.5 186.3 %copy-start = (bf16[256,1024]{1,0:T(8,128)(2,1)S(1)}, bf16[256,1024]{1,0:T(8,128)(2,1)}, u32[]{:S(2)}) copy-start(bf16[256,1024]{1,0:T(8,128)(2,1)} %param.13) | copy-start | bytes 1572868
  6.5 12.0 %copy-start.3 = (bf16[2,32,8]{1,2,0:T(8,128)(2,1)S(1)}, bf16[2,32,8]{1,2,0:T(8,128)(2,1)}, u32[]{:S(2)}) copy-start(bf16[2,32,8]{1,2,0:T(8,128)(2,1)} %param.9) | copy-start | bytes 3076
  18.6 13.8 %copy-start.2 = (bf16[1,8192]{1,0:T(2,128)(2,1)S(1)}, bf16[1,8192]{1,0:T(2,128)(2,1)}, u32[]{:S(2)}) copy-start(bf16[1,8192]{1,0:T(2,128)(2,1)} %param.7) | copy-start | bytes 49156
  92.7 5.7 %copy-start.1 = (f32[8,2048,32,8]{1,2,3,0:T(8,128)}, f32[8,2048,32,8]{1,2,3,0:T(8,128)S(1)}, u32[]{:S(2)}) copy-start(f32[8,2048,32,8]{1,2,3,0:T(8,128)S(1)} %get-tuple-element.15) | copy-start | bytes 50331652
  102.9 17.1 %all-to-all-start.2 = ((f32[32,8,8]{2,1,0:T(8,128)}), f32[32,8,8]{2,1,0:T(8,128)S(1)}, u32[]{:S(2)}, u32[]{:S(2)}) async-start(f32[32,8,8]{2,1,0:T(8,128)} %copy.42), calls=%async_computation.2 | async-start | bytes 262144 | tf_op jit(solution)/shard_map/all_to_all | solution.py:85
  120.0 15.5 %all-to-all-start.1 = ((f32[32,8,8]{2,1,0:T(8,128)}), f32[32,8,8]{2,1,0:T(8,128)S(1)}, u32[]{:S(2)}, u32[]{:S(2)}) async-start(f32[32,8,8]{2,1,0:T(8,128)} %copy.37), calls=%async_computation.1 | async-start | bytes 262144 | tf_op jit(solution)/shard_map/all_to_all | solution.py:84
  135.5 27.7 %all-to-all-start = ((f32[32,8,8,128]{3,2,1,0:T(8,128)}), f32[32,8,8,128]{3,2,1,0:T(8,128)S(1)}, u32[]{:S(2)}, u32[]{:S(2)}) async-start(f32[32,8,8,128]{3,2,1,0:T(8,128)} %copy.36), calls=%async_computation | async-start | bytes 2097152 | tf_op jit(solution)/shard_map/all_to_all | solution.py:83
  145.3 257.1 %reduce-scatter.2.cloned.1.call-start = ((), (), s32[]{:S(2)}) async-start(), calls=%async_computation.5 | async-start | bytes 1081344 | tf_op jit(solution)/shard_map/reduce_scatter | solution.py:99
Sparse Core Ops, SparseCore 0:
  194.2 208.0 reduce-scatter.1
where the time goes:
time: 412 us; the launch traced here: 411 us
  waiting for transfers between devices  227 us (55%)
  blocking collectives  80 us (19%)
  other arithmetic  30.7 us (7%)
  starting transfers between devices  21.4 us (5%)
  local copies, waits for them, and re-layouts  19.3 us (5%)
  matrix products  16.9 us (4%)
  between operations  14.9 us (4%)
    reduce_scatter x1, waiting for transfers between devices, body(): lax.psum_scatter(jnp.dot(all_rows, w_out, preferred_element_type=jnp.floa...  208 us
    all_gather x1, blocking collectives, body(): collected_rows = lax.all_gather(query, 'prefix', axis=0, tiled=True)  52.4 us
    all_to_all x1, blocking collectives, body(): lax.all_to_all(attention, 'prefix', split_axis=1, concat_axis=0, tiled=True)  14.4 us
    all_gather x1, blocking collectives, body(): all_rows = lax.all_gather(regrouped, 'samples', axis=0, tiled=True)  13.1 us
    reshape x1, other arithmetic, body(): prompt_code_cache.astype(jnp.float32)  11.3 us
    all_to_all x1, starting transfers between devices, body(): lax.all_to_all(block_out, 'prefix', split_axis=0, concat_axis=0, tiled=True)  9.79 us
    all_to_all x1, waiting for transfers between devices, body(): lax.all_to_all(block_out, 'prefix', split_axis=0, concat_axis=0, tiled=True)  9.66 us
    convert_element_type x1, other arithmetic, body(): matrix_product.astype(jnp.bfloat16)  9.57 us
  transfers between devices with their start and end apart: 4, of which 3 were waited for; matrix products, arithmetic and copies ran while one was open for 5% of the time, Pallas kernels for 0%

commit v1 on v0

v1 whole, which is shorter than its diff:
```python
import math, functools
import jax, jax.numpy as jnp
from jax import lax
from jax.experimental import pallas as pl
from jax.experimental.pallas import tpu as pltpu
from jax.sharding import PartitionSpec as P

LOG2E = 1.4426950408889634

def prep_kernel(n_ref, sc_ref, code_ref, k_ref, v_ref, x_s, k0_s, *, tb, sb):
    i = pl.program_id(0)
    heads = code_ref.shape[2]
    lanes = code_ref.shape[3]
    n = n_ref[0]
    row = lax.broadcasted_iota(jnp.int32, (sb, lanes), 0)
    for b in range(tb // sb):
        t0 = i * tb + b * sb
        ok = row < n - t0
        blk = i * (tb // sb) + b
        for c in range(2):
            x = code_ref[c, b * sb:(b + 1) * sb].astype(jnp.float32)
            x_s[c] = x.reshape(sb * heads, lanes)
            for j in range(heads):
                y = x_s[c, pl.ds(j, sb, stride=heads), :]
                y = y * sc_ref[c, blk * heads + j]
                if c == 0:
                    if b == 0:
                        @pl.when(i == 0)
                        def _():
                            k0_s[j] = jnp.broadcast_to(y[0:1], (8, lanes))
                    y = jnp.where(ok, y, k0_s[j, 0:1])
                    k_ref[j, b * sb:(b + 1) * sb, :] = y.astype(jnp.bfloat16)
                else:
                    y = jnp.where(ok, y, 0.0)
                    v_ref[j, b * sb:(b + 1) * sb, 0:lanes] = y.astype(jnp.bfloat16)
                    v_ref[j, b * sb:(b + 1) * sb, lanes:2 * lanes] = jnp.where(ok, 1.0, 0.0).astype(jnp.bfloat16)

def prep(n, scale, code, tb=256):
    _, T, H, D = code.shape
    sb = T // scale.shape[1]
    sc = scale.astype(jnp.float32).reshape(2, -1)
    return pl.pallas_call(
        functools.partial(prep_kernel, tb=tb, sb=sb),
        grid=(T // tb,),
        in_specs=[pl.BlockSpec(memory_space=pltpu.SMEM), pl.BlockSpec(memory_space=pltpu.SMEM),
                  pl.BlockSpec((2, tb, H, D), lambda i: (0, i, 0, 0))],
        out_specs=[pl.BlockSpec((H, tb, D), lambda i: (0, i, 0)), pl.BlockSpec((H, tb, 2 * D), lambda i: (0, i, 0))],
        out_shape=[jax.ShapeDtypeStruct((H, T, D), jnp.bfloat16), jax.ShapeDtypeStruct((H, T, 2 * D), jnp.bfloat16)],
        scratch_shapes=[pltpu.VMEM((2, sb * H, D), jnp.float32), pltpu.VMEM((H, 8, D), jnp.float32)],
        compiler_params=pltpu.CompilerParams(vmem_limit_bytes=40 << 20),
        cost_estimate=pl.CostEstimate(flops=16 << 20, bytes_accessed=20 << 20, transcendentals=0),
        name="prep",
    )(n, sc, code)

def suffix_kernel(len_ref, q_ref, c_ref, o_ref, m_ref, t_ref, *, cs):
    T = c_ref.shape[2]
    D = q_ref.shape[1]
    H = c_ref.shape[3] // D
    G = q_ref.shape[0] // H
    length = len_ref[0]
    valid = lax.broadcasted_iota(jnp.int32, (G, T), 1) < length
    q = q_ref[...].astype(jnp.float32)
    for j in range(H):
        qj = q[j * G:(j + 1) * G].astype(jnp.bfloat16)
        s = lax.dot_general(qj, c_ref[0, 0, :, j * D:(j + 1) * D], (((1,), (1,)), ((), ())), preferred_element_type=jnp.float32) * cs
        s = jnp.where(valid, s, -jnp.inf)
        m = jnp.max(s, axis=1, keepdims=True)
        w = jnp.exp2(s - m).astype(jnp.bfloat16)
        t = jnp.sum(w.astype(jnp.float32), axis=1, keepdims=True)
        o = jnp.dot(w, c_ref[0, 1, :, j * D:(j + 1) * D], preferred_element_type=jnp.float32)
        o_ref[j * G:(j + 1) * G, :] = o
        m_ref[j * G:(j + 1) * G, :] = jnp.broadcast_to(m, (G, D))
        t_ref[j * G:(j + 1) * G, :] = jnp.broadcast_to(t, (G, D))

def suffix(length, q, cache):
    HQ, D = q.shape
    return pl.pallas_call(
        functools.partial(suffix_kernel, cs=LOG2E / math.sqrt(D)),
        in_specs=[pl.BlockSpec(memory_space=pltpu.SMEM), pl.BlockSpec(memory_space=pltpu.VMEM), pl.BlockSpec(memory_space=pltpu.VMEM)],
        out_specs=[pl.BlockSpec(memory_space=pltpu.VMEM)] * 3,
        out_shape=[jax.ShapeDtypeStruct((HQ, D), jnp.float32)] * 3,
        compiler_params=pltpu.CompilerParams(vmem_limit_bytes=40 << 20),
        cost_estimate=pl.CostEstimate(flops=1 << 27, bytes_accessed=2 << 20, transcendentals=0),
        name="suffix",
    )(length, q, cache)

def attn_kernel(meta_ref, qg_ref, k_ref, v_ref, so_ref, sm_ref, st_ref, out_ref, q_s, *, cs, rows, k_heads):
    j = pl.program_id(0)
    S, HQ, D = qg_ref.shape
    H = pl.num_programs(0)
    G = HQ // k_heads
    n = meta_ref[0]
    me = meta_ref[1]
    @pl.when(j == 0)
    def _():
        q_s[...] = qg_ref[...].astype(jnp.float32).reshape(S * HQ, D)
    R = G * S
    hp = 64 // S
    sidx = lax.broadcasted_iota(jnp.int32, (S, D), 0)
    neg = -(2.0 ** 127)
    for r in range(R // rows):
        hs = rows // S
        q = jnp.concatenate([q_s[pl.ds(j * G + r * hs + h, S, stride=HQ), :] for h in range(hs)], axis=0).astype(jnp.bfloat16)
        z = lax.dot_general(q, k_ref[0], (((1,), (1,)), ((), ())), preferred_element_type=jnp.float32)
        m = jnp.max(z, axis=1, keepdims=True) * cs
        m = jnp.broadcast_to(m, (rows, D))
        m = m.astype(jnp.bfloat16).astype(jnp.float32)
        p = jnp.exp2(z * cs - m[:, 0:1]).astype(jnp.bfloat16)
        o = jnp.dot(p, v_ref[0], preferred_element_type=jnp.float32)
        tot = o[:, D:]
        o = o[:, :D]
        m = jnp.where(n > 0, m, neg)
        mts = []
        for h in range(hs):
            hh = r * hs + h
            sl = slice(h * S, (h + 1) * S)
            so = so_ref[pl.ds(j * G + hh, 1), :]
            sm = sm_ref[pl.ds(j * G + hh, 1), :]
            st = st_ref[pl.ds(j * G + hh, 1), :]
            mine = sidx == me
            sm2 = jnp.where(mine, sm, neg)
            mn = jnp.maximum(m[sl], sm2).astype(jnp.bfloat16).astype(jnp.float32)
            fa = jnp.exp2(m[sl] - mn)
            fb = jnp.where(mine, jnp.exp2(sm2 - mn), 0.0)
            on = o[sl] * fa + so * fb
            tn = tot[sl] * fa + st * fb
            d, hd = divmod(hh, hp)
            out_ref[d, hd * S:(hd + 1) * S, :] = on.astype(jnp.bfloat16)
            mts.append((mn, tn))
        for d0 in range(hs // hp):
            mm = jnp.concatenate([a for a, _ in mts[d0 * hp:(d0 + 1) * hp]], axis=0)
            tt = jnp.concatenate([b for _, b in mts[d0 * hp:(d0 + 1) * hp]], axis=0)
            diag = lax.broadcasted_iota(jnp.int32, (64, D), 0) == lax.broadcasted_iota(jnp.int32, (64, D), 1)
            mr = jnp.sum(jnp.where(diag, mm, 0.0), axis=0, keepdims=True)
            tr = jnp.sum(jnp.where(diag, tt, 0.0), axis=0, keepdims=True)
            hi = tr.astype(jnp.bfloat16).astype(jnp.float32)
            lo = tr - hi
            st = jnp.concatenate([mr, hi, lo, jnp.zeros((13, D), jnp.float32)], axis=0)
            out_ref[(r * hs) // hp + d0, 64:80, :] = st.astype(jnp.bfloat16)

def attn(meta, qg, k, v, so, sm, st, rows=256):
    S, HQ, D = qg.shape
    H, T, _ = k.shape
    nd = HQ * S // 64
    whole = lambda shape: pl.BlockSpec(shape, lambda j: (0,) * len(shape))
    return pl.pallas_call(
        functools.partial(attn_kernel, cs=LOG2E / math.sqrt(D), rows=rows, k_heads=H),
        grid=(H,),
        in_specs=[pl.BlockSpec(memory_space=pltpu.SMEM), whole(qg.shape),
                  pl.BlockSpec((1, T, D), lambda j: (j, 0, 0)), pl.BlockSpec((1, T, 2 * D), lambda j: (j, 0, 0)),
                  whole(so.shape), whole(sm.shape), whole(st.shape)],
        out_specs=pl.BlockSpec((nd // H, 80, D), lambda j: (j, 0, 0)),
        out_shape=jax.ShapeDtypeStruct((nd, 80, D), jnp.bfloat16),
        scratch_shapes=[pltpu.VMEM((S * HQ, D), jnp.float32)],
        compiler_params=pltpu.CompilerParams(vmem_limit_bytes=48 << 20),
        cost_estimate=pl.CostEstimate(flops=2 << 30, bytes_accessed=12 << 20, transcendentals=4 << 20),
        name="attn",
    )(meta, qg, k, v, so, sm, st)

def combine_kernel(r_ref, o_ref, st_s):
    B = r_ref.shape[0]
    D = r_ref.shape[2]
    st_s[...] = r_ref[:, 64:80, :].astype(jnp.float32).reshape(B * 16, D)
    m = st_s[pl.ds(0, B, stride=16), :]
    t = st_s[pl.ds(1, B, stride=16), :] + st_s[pl.ds(2, B, stride=16), :]
    M = jnp.max(m, axis=0, keepdims=True)
    f = jnp.exp2(m - M)
    den = jnp.sum(f * t, axis=0, keepdims=True)
    lane = lax.broadcasted_iota(jnp.int32, (B, D), 1)
    f = jnp.where(lane < 64, f / den, 0.0)
    ft = jnp.transpose(jnp.concatenate([f, jnp.zeros((D - B, D), jnp.float32)], axis=0))[:64]
    acc = jnp.zeros((64, D), jnp.float32)
    for b in range(B):
        acc = acc + r_ref[b, 0:64, :].astype(jnp.float32) * ft[:, b:b + 1]
    res = jnp.concatenate([acc[:32], acc[32:]], axis=1).astype(jnp.bfloat16)
    for g in range(o_ref.shape[0]):
        o_ref[g] = res

def combine(r, copies):
    B, _, D = r.shape
    return pl.pallas_call(
        combine_kernel,
        in_specs=[pl.BlockSpec(memory_space=pltpu.VMEM)],
        out_specs=pl.BlockSpec(memory_space=pltpu.VMEM),
        out_shape=jax.ShapeDtypeStruct((copies, 32, 2 * D), jnp.bfloat16),
        scratch_shapes=[pltpu.VMEM((B * 16, D), jnp.float32)],
        compiler_params=pltpu.CompilerParams(vmem_limit_bytes=40 << 20),
        cost_estimate=pl.CostEstimate(flops=1 << 20, bytes_accessed=1 << 20, transcendentals=0),
        name="combine",
    )(r)

def body(query, prompt_code_cache, prompt_scale_cache, prefix_len, sample_key_value_cache, suffix_len, w_out):
    chunk = prompt_code_cache.shape[1]
    head_width = prompt_code_cache.shape[3]
    heads = query.shape[1] // head_width
    members = lax.axis_size("prefix")
    groups = lax.axis_size("samples")
    me = lax.axis_index("prefix").astype(jnp.int32)
    valid = jnp.clip(prefix_len - me * chunk, 0, chunk)

    def swap(x, axis):
        return lax.all_to_all(x, axis, split_axis=0, concat_axis=0, tiled=True)

    own = query.reshape(heads, head_width)
    gathered = swap(jnp.broadcast_to(own[None], (members, heads, head_width)), "prefix")
    keys, values = prep(valid, prompt_scale_cache, prompt_code_cache)
    so, sm, st = suffix(suffix_len, own, sample_key_value_cache)
    meta = jnp.concatenate([valid, me[None]])
    partials = attn(meta, gathered, keys, values, so, sm, st)
    attention = combine(swap(partials, "prefix"), groups)
    rows = swap(attention, "samples").reshape(-1, attention.shape[2])
    terms = jnp.dot(rows, w_out, preferred_element_type=jnp.float32).astype(jnp.bfloat16)
    terms = swap(terms.reshape(members, -1, terms.shape[1]), "prefix")
    return jnp.sum(terms.astype(jnp.float32), axis=0).astype(jnp.bfloat16)


def solution(mesh):
    in_specs = (
        P(("samples", "prefix"), None),
        P(None, "prefix", None, None),
        P(None, "prefix", None),
        P(),
        P(("samples", "prefix"), None, None, None),
        P(("samples", "prefix")),
        P("prefix", "samples"),
    )
    return jax.shard_map(body, mesh=mesh, in_specs=in_specs, out_specs=P("prefix", "samples"), check_vma=False)
```

time: 412 us -> 110 us (0.27)
  waiting for transfers between devices: 227 us -> 0.01 us
  other arithmetic: 30.7 us -> 1.77 us
  Pallas kernels: 0 us -> 24.2 us
  blocking collectives: 80 us -> 61.3 us
  matrix products: 16.9 us -> 0.3 us
  between operations: 14.9 us -> 1.37 us
  local copies, waits for them, and re-layouts: 19.3 us -> 9.16 us
  starting transfers between devices: 21.4 us -> 11.4 us
    reduce_scatter x1 -> x0, waiting for transfers between devices: 208 us -> none  [body(): lax.psum_scatter(jnp.dot(all_rows, w_out, preferred_element_type=jnp.floa...]
    all_gather x2 -> x0, blocking collectives: 65.6 us -> none  [the longest x1 52.4 us: body(): collected_rows = lax.all_gather(query, 'prefix', axis=0, tiled=True)]
    all_to_all x1 -> x3, blocking collectives: 14.4 us -> 61.3 us  [swap(): return lax.all_to_all(x, axis, split_axis=0, concat_axis=0, tiled=True)]
    pallas_call x0 -> x4, Pallas kernels: none -> 24.2 us  [the longest x1 12.7 us: attn(): pl.pallas_call(functools.partial(attn_kernel, cs=LOG2E / math.sqrt(D), ro...]
    all_to_all x3 -> x1, waiting for transfers between devices: 19.1 us -> 0.01 us  [swap(): return lax.all_to_all(x, axis, split_axis=0, concat_axis=0, tiled=True)]
    dot_general x5 -> x1, matrix products: 16.9 us -> 0.3 us  [body(): jnp.dot(rows, w_out, preferred_element_type=jnp.float32)]
    reshape x1 -> x0, other arithmetic: 11.3 us -> none  [body(): prompt_code_cache.astype(jnp.float32)]
    convert_element_type x3 -> x0, other arithmetic: 10.9 us -> none  [the longest x1 9.57 us: body(): matrix_product.astype(jnp.bfloat16)]
  transfers between devices with their start and end apart: 4 -> 1, of which waited for: 3 -> 0; matrix products, arithmetic and copies ran while one was open for 5% -> 1% of each run, Pallas kernels for 0% -> 10%
where the time goes in v1:
time: 110 us; the launch traced here: 109 us
  blocking collectives  61.3 us (56%)
  Pallas kernels  24.2 us (22%)
  starting transfers between devices  11.4 us (10%)
  local copies, waits for them, and re-layouts  9.16 us (8%)
  other arithmetic  1.77 us (2%)
  between operations  1.37 us (1%)
    all_to_all x3, blocking collectives, swap(): return lax.all_to_all(x, axis, split_axis=0, concat_axis=0, tiled=True)  61.3 us
    pallas_call x1, Pallas kernels, attn(): pl.pallas_call(functools.partial(attn_kernel, cs=LOG2E / math.sqrt(D), ro...  12.7 us
    all_to_all x1, starting transfers between devices, swap(): return lax.all_to_all(x, axis, split_axis=0, concat_axis=0, tiled=True)  11.4 us
    pallas_call x1, Pallas kernels, prep(): pl.pallas_call(functools.partial(prep_kernel, tb=tb, sb=sb), grid=(T // t...  8.91 us
    unnamed x10, local copies, waits for them, and re-layouts  7.36 us
  transfers between devices with their start and end apart: 1, of which 0 were waited for; matrix products, arithmetic and copies ran while one was open for 1% of the time, Pallas kernels for 10%

profile of v1, /device:TPU:32, one launch (start us, length us, event | category | flops | bytes accessed | tf_op | source)
XLA Modules:
  0.0 109.4 jit_solution(17108613948281263442)
XLA Ops:
  0.0 0.0 copy-start
  0.0 0.0 copy-start.4
  0.0 1.0 reduce.1
  1.0 0.9 broadcast_in_dim.12
  1.9 11.4 %all-to-all-start = ((bf16[32,64,128]{2,1,0:T(8,128)(2,1)}), bf16[32,64,128]{2,1,0:T(8,128)(2,1)S(1)}, u32[]{:S(2)}, u32[]{:S(2)}) async-start(bf16[32,64,128]{2,1,0:T(8,128)(2,1)} %broadcast_in_dim.12), calls=%async_computation | async-start | bytes 1048576 | tf_op jit(solution)/shard_map/all_to_all | solution.py:202
  14.6 0.8 copy.9
  15.4 0.1 reshape.18.sc_ref
  15.5 8.9 %prep.1 = (bf16[8,2048,128]{2,1,0:T(8,128)(2,1)S(1)}, bf16[8,2048,256]{2,1,0:T(8,128)(2,1)S(1)}) custom-call(s32[1]{0:T(128)S(6)} %min.6.n_ref, f32[2,256]{1,0:T(2,128)S(1)} %reshape.18.sc_ref, bf16[2,2048,8,128]{3,2,1,0:T(8,128)(2,1)} %code_ref.1), custom_call_target="tpu_custom_call" | custom-call | flops 16777216 | bytes 20971520 | tf_op jit(solution)/shard_map/prep/pallas_call | solution.py:42
  24.4 0.0 copy-start.1
  24.4 3.2 %copy-done.1 = bf16[8,2048,256]{2,1,0:T(8,128)(2,1)} copy-done((bf16[8,2048,256]{2,1,0:T(8,128)(2,1)}, bf16[8,2048,256]{2,1,0:T(8,128)(2,1)S(1)}, u32[]{:S(2)}) %copy-start.1) | copy-done | bytes 8388632
  27.6 0.0 copy-start.2
  27.6 1.9 %copy-done.2 = bf16[8,2048,128]{2,1,0:T(8,128)(2,1)} copy-done((bf16[8,2048,128]{2,1,0:T(8,128)(2,1)}, bf16[8,2048,128]{2,1,0:T(8,128)(2,1)S(1)}, u32[]{:S(2)}) %copy-start.2) | copy-done | bytes 4194328
  29.6 0.0 copy-done.4
  29.6 2.0 %suffix.1 = (f32[64,128]{1,0:T(8,128)S(1)}, f32[64,128]{1,0:T(8,128)S(1)}, f32[64,128]{1,0:T(8,128)S(1)}) custom-call(s32[1]{0:T(128)S(6)} %copy.11.len_ref, bf16[64,128]{1,0:T(8,128)(2,1)S(1)} %bitcast.9, bf16[1,2,512,1024]{3,2,1,0:T(8,128)(2,1)S(1)} %copy-done.4), custom_call_target="tpu_custom_call" | custom-call | flops 134217728 | bytes 2097152 | tf_op jit(solution)/shard_map/suffix/pallas_call | solution.py:77
  31.6 0.1 pad_add_fusion.meta_ref
  31.6 0.0 all-to-all-done.qg_ref
  31.6 0.0 copy-start.3
  31.6 2.2 %copy-done.3 = bf16[8,2048,128]{2,1,0:T(8,128)(2,1)S(1)} copy-done((bf16[8,2048,128]{2,1,0:T(8,128)(2,1)S(1)}, bf16[8,2048,128]{2,1,0:T(8,128)(2,1)}, u32[]{:S(2)}) %copy-start.3) | copy-done | bytes 4194328
  33.8 12.7 %attn.1 = bf16[32,80,128]{2,1,0:T(8,128)(2,1)S(1)} custom-call(s32[2]{0:T(128)S(1)} %pad_add_fusion.meta_ref, bf16[32,64,128]{2,1,0:T(8,128)(2,1)S(1)} %all-to-all-done.qg_ref, bf16[8,2048,128]{2,1,0:T(8,128)(2,1)S(1)} %copy-done.3, bf16[8,2048,256]{2,1,0:T(8,128)(2,1)} %copy-done.1, f32[64,128]{1,0:T(8,128)S(1)} %get-tuple-element.12.so_ref, ...), custom_call_target="tpu_custom_call" | custom-call | flops 2147483648 | bytes 12582912 | tf_op jit(solution)/shard_map/attn/pallas_call | solution.py:146
  46.6 28.8 %all_to_all.20.r_ref = bf16[32,80,128]{2,1,0:T(8,128)(2,1)S(1)} all-to-all(bf16[32,80,128]{2,1,0:T(8,128)(2,1)S(1)} %attn.1), channel_id=1, replica_groups=mesh['prefix'=32,'samples'=8] {'prefix'}, dimensions={0} | all-to-all | bytes 1310720 | tf_op jit(solution)/shard_map/all_to_all | solution.py:202
  75.4 0.6 combine.1
  75.9 10.2 %all_to_all.21 = bf16[8,32,256]{2,1,0:T(8,128)(2,1)S(1)} all-to-all(bf16[8,32,256]{2,1,0:T(8,128)(2,1)S(1)} %combine.1), channel_id=1, replica_groups=mesh['prefix'=32,'samples'=8] {'samples'}, dimensions={0} | all-to-all | bytes 262144 | tf_op jit(solution)/shard_map/all_to_all | solution.py:202
  86.2 0.0 copy-done
  86.2 0.3 fusion
  86.5 22.2 %all_to_all.22 = bf16[32,8,1024]{2,1,0:T(8,128)(2,1)S(1)} all-to-all(bf16[32,8,1024]{2,1,0:T(8,128)(2,1)S(1)} %fusion), channel_id=1, replica_groups=mesh['prefix'=32,'samples'=8] {'prefix'}, dimensions={0} | all-to-all | bytes 1048576 | tf_op jit(solution)/shard_map/all_to_all | solution.py:202
  108.7 0.7 reduce_sum.12
Async XLA Ops:
  0.0 86.2 %copy-start = (bf16[256,1024]{1,0:T(8,128)(2,1)S(1)}, bf16[256,1024]{1,0:T(8,128)(2,1)}, u32[]{:S(2)}) copy-start(bf16[256,1024]{1,0:T(8,128)(2,1)} %param.13) | copy-start | bytes 1572868
  0.0 29.6 %copy-start.4 = (bf16[1,2,512,1024]{3,2,1,0:T(8,128)(2,1)S(1)}, bf16[1,2,512,1024]{3,2,1,0:T(8,128)(2,1)}, u32[]{:S(2)}) copy-start(bf16[1,2,512,1024]{3,2,1,0:T(8,128)(2,1)} %c_ref.1) | copy-start | bytes 6291460
  1.9 29.7 %all-to-all-start = ((bf16[32,64,128]{2,1,0:T(8,128)(2,1)}), bf16[32,64,128]{2,1,0:T(8,128)(2,1)S(1)}, u32[]{:S(2)}, u32[]{:S(2)}) async-start(bf16[32,64,128]{2,1,0:T(8,128)(2,1)} %broadcast_in_dim.12), calls=%async_computation | async-start | bytes 1048576 | tf_op jit(solution)/shard_map/all_to_all | solution.py:202
  24.4 3.2 %copy-start.1 = (bf16[8,2048,256]{2,1,0:T(8,128)(2,1)}, bf16[8,2048,256]{2,1,0:T(8,128)(2,1)S(1)}, u32[]{:S(2)}) copy-start(bf16[8,2048,256]{2,1,0:T(8,128)(2,1)S(1)} %get-tuple-element.11.v_ref) | copy-start | bytes 25165828
  27.6 1.9 %copy-start.2 = (bf16[8,2048,128]{2,1,0:T(8,128)(2,1)}, bf16[8,2048,128]{2,1,0:T(8,128)(2,1)S(1)}, u32[]{:S(2)}) copy-start(bf16[8,2048,128]{2,1,0:T(8,128)(2,1)S(1)} %get-tuple-element.10.k_ref) | copy-start | bytes 12582916
  31.6 2.2 %copy-start.3 = (bf16[8,2048,128]{2,1,0:T(8,128)(2,1)S(1)}, bf16[8,2048,128]{2,1,0:T(8,128)(2,1)}, u32[]{:S(2)}) copy-start(bf16[8,2048,128]{2,1,0:T(8,128)(2,1)} %copy-done.2) | copy-start | bytes 12582916

commit v2 on v1

v2 whole, which is shorter than its diff:
```python
import math, functools
import jax, jax.numpy as jnp
from jax import lax
from jax.experimental import pallas as pl
from jax.experimental.pallas import tpu as pltpu
from jax.sharding import PartitionSpec as P
LOG2E = 1.4426950408889634
FLOOR = -(2.0 ** 127)

def prep_kernel(n_ref, len_ref, sc_ref, code_hbm, q_ref, cache_hbm, k_hbm, v_hbm, own_ref, code_s, cache_s, k_s, v_s, hot_s, in_sem, cache_sem, k_sem, v_sem, *, tb, sb, cs):
    H, _, lanes = k_s.shape
    G = own_ref.shape[1] // H
    steps = k_s.shape[1] // tb

    def rows(i, size):
        return pl.ds(pl.multiple_of(i * size, size), size)

    def load(i):
        return pltpu.make_async_copy(code_hbm.at[:, rows(i, tb * H), :], code_s.at[:, rows(i, tb * H), :], in_sem.at[i])

    def save(i):
        at = rows(i, tb)
        return (pltpu.make_async_copy(k_s.at[:, at, :], k_hbm.at[:, at, :], k_sem.at[i]),
                pltpu.make_async_copy(v_s.at[:, at, :], v_hbm.at[:, at, :], v_sem.at[i]))

    cache_copy = pltpu.make_async_copy(cache_hbm, cache_s, cache_sem)
    load(0).start()
    cache_copy.start()
    for i in range(1, steps):
        load(i).start()
    hr = hot_s.shape[0]
    half = sb // 2
    r = lax.broadcasted_iota(jnp.int32, (hr, hr), 0)
    c = lax.broadcasted_iota(jnp.int32, (hr, hr), 1)
    hot_s[...] = jnp.where((r % half) * H + r // half == c, 1.0, 0.0).astype(jnp.bfloat16)

    @pl.loop(0, steps)
    def _(i):
        load(i).wait()
        prep_step(i, n_ref, sc_ref, code_s, k_s, v_s, hot_s, tb=tb, sb=sb)
        for copy in save(i):
            copy.start()

    cache_copy.wait()
    q = q_ref[...].astype(jnp.float32)
    for i in range(H):
        own = jnp.concatenate([q[:, h * lanes:(h + 1) * lanes] for h in range(i * G, (i + 1) * G)], axis=0).astype(jnp.bfloat16)
        cols = slice(i * lanes, (i + 1) * lanes)
        grp = slice(i * G, (i + 1) * G)
        T = cache_s.shape[2]
        s = lax.dot_general(own, cache_s[0, 0, :, cols], (((1,), (1,)), ((), ())), preferred_element_type=jnp.float32) * cs
        s = jnp.where(lax.broadcasted_iota(jnp.int32, (G, T), 1) < len_ref[0], s, -jnp.inf)
        m = jnp.max(s, axis=1, keepdims=True)
        w = jnp.exp2(s - m).astype(jnp.bfloat16)
        own_ref[0, grp, :] = jnp.dot(w, cache_s[0, 1, :, cols], preferred_element_type=jnp.float32)
        own_ref[1, grp, :] = jnp.broadcast_to(m, (G, lanes))
        own_ref[2, grp, :] = jnp.broadcast_to(jnp.sum(w.astype(jnp.float32), axis=1, keepdims=True), (G, lanes))
    for i in range(steps):
        for copy in save(i):
            copy.wait()


def prep_step(i, n_ref, sc_ref, code_ref, k_ref, v_ref, hot_s, *, tb, sb):
    heads = k_ref.shape[0]
    lanes = code_ref.shape[2]
    half = sb // 2
    hr = half * heads
    n = n_ref[0]

    def move(c, b):
        x = jnp.concatenate([code_ref[c, pl.ds(pl.multiple_of(i * tb * heads, tb * heads) + (2 * b + u) * hr, hr), :] for u in range(2)], axis=1)
        y = jnp.dot(hot_s[...], x, preferred_element_type=jnp.float32)
        blk = i * (tb // sb) + b
        return [y[j * half:(j + 1) * half] * sc_ref[c, blk * heads + j] for j in range(heads)]

    def go(masked):
        for b in range(tb // sb):
            rows = [pl.ds(pl.multiple_of(i * tb, tb) + b * sb + u * half, half) for u in range(2)]
            if masked:
                left = n - i * tb - b * sb
                ok = [lax.broadcasted_iota(jnp.int32, (half, lanes), 0) + u * half < left for u in range(2)]
            for c in range(2):
                ys = move(c, b)
                if masked and c == 0 and b == 0:
                    first = [y[0:1, 0:lanes] for y in ys]
                for j in range(heads):
                    for u in range(2):
                        y = ys[j][:, u * lanes:(u + 1) * lanes]
                        if c == 0:
                            if masked:
                                y = jnp.where(ok[u], y, first[j])
                            k_ref[j, rows[u], :] = y.astype(jnp.bfloat16)
                        else:
                            if masked:
                                y = jnp.where(ok[u], y, 0.0)
                            v_ref[j, rows[u], :] = y.astype(jnp.bfloat16)

    whole = (i + 1) * tb <= n
    some = i * tb < n

    @pl.when(whole)
    def _():
        go(False)

    @pl.when(jnp.logical_and(some, jnp.logical_not(whole)))
    def _():
        go(True)

    @pl.when(jnp.logical_not(some))
    def _():
        for j in range(heads):
            k_ref[j, pl.ds(pl.multiple_of(i * tb, tb), tb), :] = jnp.broadcast_to(jnp.where(i == 0, 0.0, k_ref[j, 0:16].astype(jnp.float32)[0:1]), (tb, lanes)).astype(jnp.bfloat16)
            v_ref[j, pl.ds(pl.multiple_of(i * tb, tb), tb), :] = jnp.zeros((tb, lanes), jnp.bfloat16)

def prep(n, length, scale, code, q, cache):
    _, T, H, D = code.shape
    tb = T // 4
    sb = T // scale.shape[1]
    G = q.shape[1] // (H * D)
    sc = scale.astype(jnp.float32).reshape(2, -1)
    smem = pl.BlockSpec(memory_space=pltpu.SMEM)
    vmem = pl.BlockSpec(memory_space=pltpu.VMEM)
    hbm = pl.BlockSpec(memory_space=pltpu.HBM)
    return pl.pallas_call(
        functools.partial(prep_kernel, tb=tb, sb=sb, cs=LOG2E / math.sqrt(D)),
        in_specs=[smem, smem, smem, hbm, vmem, hbm],
        out_specs=[hbm, hbm, vmem],
        out_shape=[jax.ShapeDtypeStruct((H, T, D), jnp.bfloat16)] * 2 + [jax.ShapeDtypeStruct((3, H * G, D), jnp.float32)],
        scratch_shapes=[pltpu.VMEM((2, T * H, D), jnp.bfloat16), pltpu.VMEM(cache.shape, jnp.bfloat16),
                        pltpu.VMEM((H, T, D), jnp.bfloat16), pltpu.VMEM((H, T, D), jnp.bfloat16),
                        pltpu.VMEM((sb // 2 * H, sb // 2 * H), jnp.bfloat16),
                        pltpu.SemaphoreType.DMA((T // tb,)), pltpu.SemaphoreType.DMA,
                        pltpu.SemaphoreType.DMA((T // tb,)), pltpu.SemaphoreType.DMA((T // tb,))],
        compiler_params=pltpu.CompilerParams(vmem_limit_bytes=63_300_000),
        cost_estimate=pl.CostEstimate(flops=16 << 20, bytes_accessed=20 << 20, transcendentals=0),
        name="prep",
    )(n, length, sc, code.reshape(2, T * H, D), q, cache)

def attn_kernel(n_ref, me_ref, qg_hbm, k_hbm, v_hbm, own_hbm, out_ref, qg_ref, own_ref, qg_sem, own_sem, q_s, k_ref, v_ref, one_s, k_sem, v_sem, *s_s, cs, tile, nbuf):
    S, HQ, D = qg_ref.shape
    H, T, _ = k_hbm.shape
    G = HQ // H
    n = n_ref[0]
    me = me_ref[0]
    R = G * S
    hp = 64 // S
    load_k = [pltpu.make_async_copy(k_hbm.at[j], k_ref.at[j], k_sem.at[j]) for j in range(H)]
    load_v = [pltpu.make_async_copy(v_hbm.at[j], v_ref.at[j], v_sem.at[j]) for j in range(H)]
    load_own = pltpu.make_async_copy(own_hbm, own_ref, own_sem)
    load_q = pltpu.make_async_copy(qg_hbm, qg_ref, qg_sem)
    load_q.start()
    load_k[0].start()
    load_k[1].start()
    load_v[0].start()
    load_own.start()
    one_s[...] = jnp.where(lax.broadcasted_iota(jnp.int32, (T, D), 0) < n, 1.0, 0.0).astype(jnp.bfloat16)
    sidx = lax.broadcasted_iota(jnp.int32, (S, D), 0)
    load_q.wait()
    q_s[...] = qg_ref[...].astype(jnp.float32).reshape(S * HQ, D)
    ms = {}
    def scores(j, c):
        if c == 0:
            q = jnp.concatenate([q_s[pl.ds(j * G + h, S, stride=HQ), :] for h in range(G)], axis=0).astype(jnp.bfloat16)
            ms[j] = [q, None]
        q = ms[j][0]
        z = lax.dot_general(q, k_ref[j, c * tile:(c + 1) * tile, :], (((1,), (1,)), ((), ())), preferred_element_type=jnp.float32)
        s_s[j % nbuf][:, c * tile:(c + 1) * tile] = z
        m = ms[j][1]
        for l in range(tile // D):
            zz = z[:, l * D:(l + 1) * D]
            m = zz if m is None else jnp.maximum(m, zz)
        ms[j][1] = m
        if (c + 1) * tile == T:
            m = jnp.max(m, axis=1, keepdims=True) * cs
            ms[j][1] = jnp.broadcast_to(m, (R, D)).astype(jnp.bfloat16).astype(jnp.float32)
    acc = {}
    def weigh(j, c):
        m = ms[j][1]
        z = s_s[j % nbuf][:, c * tile:(c + 1) * tile]
        p = jnp.exp2(z * cs - jnp.concatenate([m] * (tile // D), axis=1)).astype(jnp.bfloat16)
        at = slice(c * tile, (c + 1) * tile)
        o = jnp.dot(p, jnp.concatenate([v_ref[j, at, :], one_s[at, :]], axis=1), preferred_element_type=jnp.float32)
        acc[j] = o if c == 0 else acc[j] + o
    def finish(j):
        o = acc[j][:, :D]
        tot = acc[j][:, D:]
        m = jnp.where(n > 0, ms[j][1], FLOOR)
        mts = []
        for h in range(G):
            sl = slice(h * S, (h + 1) * S)
            r = j * G + h
            mine = sidx == me
            sm2 = jnp.where(mine, own_ref[1, r:r + 1, :], FLOOR)
            mn = jnp.maximum(m[sl], sm2).astype(jnp.bfloat16).astype(jnp.float32)
            fa = jnp.exp2(m[sl] - mn)
            fb = jnp.where(mine, jnp.exp2(sm2 - mn), 0.0)
            on = o[sl] * fa + own_ref[0, r:r + 1, :] * fb
            tn = tot[sl] * fa + own_ref[2, r:r + 1, :] * fb
            d, hd = divmod(r, hp)
            out_ref[d, hd * S:(hd + 1) * S, :] = on.astype(jnp.bfloat16)
            mts.append((mn, tn))
        diag = lax.broadcasted_iota(jnp.int32, (64, D), 0) == lax.broadcasted_iota(jnp.int32, (64, D), 1)
        for d0 in range(G // hp):
            mm = jnp.concatenate([a for a, _ in mts[d0 * hp:(d0 + 1) * hp]], axis=0)
            tt = jnp.concatenate([b for _, b in mts[d0 * hp:(d0 + 1) * hp]], axis=0)
            mr = jnp.sum(jnp.where(diag, mm, 0.0), axis=0, keepdims=True)
            tr = jnp.sum(jnp.where(diag, tt, 0.0), axis=0, keepdims=True)
            hi = tr.astype(jnp.bfloat16).astype(jnp.float32)
            st = jnp.concatenate([mr, hi, tr - hi, jnp.zeros((13, D), jnp.float32)], axis=0)
            out_ref[j * (G // hp) + d0, 64:80, :] = st.astype(jnp.bfloat16)
    nt = T // tile
    K = lambda *a: [('k', i) for i in a]
    V = lambda *a: [('v', i) for i in a]
    waits = {0: K(0), 1: K(1) + V(0), 2: K(2, 3) + V(1, 2), 4: K(4, 5) + V(3, 4), 6: K(6, 7) + V(5, 6, 7)}
    plan = {0: K(2, 3) + V(1, 2), 1: K(4, 5) + V(3, 4), 3: K(6, 7) + V(5, 6, 7)}
    for j in range(H + 1):
        for c in range(nt):
            if j < H:
                if c == 0:
                    if j == 1:
                        load_own.wait()
                    for which, i in waits.get(j, ()):
                        (load_k if which == 'k' else load_v)[i].wait()
                    for which, i in plan.get(j, ()):
                        (load_k if which == 'k' else load_v)[i].start()
                scores(j, c)
            if j == H and c == 0:
                for which, i in waits.get(j, ()):
                    (load_k if which == 'k' else load_v)[i].wait()
            if j > 0:
                weigh(j - 1, c)
        if j > 0:
            finish(j - 1)

def attn(n, me, qg, k, v, own, tile=256, nbuf=2):
    S, HQ, D = qg.shape
    H, T, _ = k.shape
    nd = HQ * S // 64
    vm = pl.BlockSpec(memory_space=pltpu.VMEM)
    hbm = pl.BlockSpec(memory_space=pltpu.HBM)
    return pl.pallas_call(
        functools.partial(attn_kernel, cs=LOG2E / math.sqrt(D), tile=tile, nbuf=nbuf),
        in_specs=[pl.BlockSpec(memory_space=pltpu.SMEM)] * 2 + [hbm] * 4,
        out_specs=vm,
        out_shape=jax.ShapeDtypeStruct((nd, 80, D), jnp.bfloat16),
        scratch_shapes=[pltpu.VMEM(qg.shape, qg.dtype), pltpu.VMEM(own.shape, own.dtype), pltpu.SemaphoreType.DMA, pltpu.SemaphoreType.DMA, pltpu.VMEM((S * HQ, D), jnp.float32), pltpu.VMEM((H, T, D), jnp.bfloat16), pltpu.VMEM((H, T, D), jnp.bfloat16), pltpu.VMEM((T, D), jnp.bfloat16),
                        pltpu.SemaphoreType.DMA((H,)), pltpu.SemaphoreType.DMA((H,))] + [pltpu.VMEM((S * HQ // H, T), jnp.float32)] * nbuf,
        compiler_params=pltpu.CompilerParams(vmem_limit_bytes=63_300_000),
        cost_estimate=pl.CostEstimate(flops=2 << 30, bytes_accessed=12 << 20, transcendentals=4 << 20),
        name="attn",
    )(n, me, qg, k, v, own)

def combine_kernel(r_ref, o_ref, st_s):
    B = r_ref.shape[0]
    D = r_ref.shape[2]
    st_s[...] = r_ref[:, 64:80, :].astype(jnp.float32).reshape(B * 16, D)
    m = st_s[pl.ds(0, B, stride=16), :]
    t = st_s[pl.ds(1, B, stride=16), :] + st_s[pl.ds(2, B, stride=16), :]
    M = jnp.max(m, axis=0, keepdims=True)
    f = jnp.exp2(m - M)
    den = jnp.sum(f * t, axis=0, keepdims=True)
    lane = lax.broadcasted_iota(jnp.int32, (B, D), 1)
    f = jnp.where(lane < 64, f / den, 0.0)
    ft = jnp.transpose(jnp.concatenate([f, jnp.zeros((D - B, D), jnp.float32)], axis=0))[:64]
    acc = jnp.zeros((64, D), jnp.float32)
    for b in range(B):
        acc = acc + r_ref[b, 0:64, :].astype(jnp.float32) * ft[:, b:b + 1]
    res = jnp.concatenate([acc[:32], acc[32:]], axis=1).astype(jnp.bfloat16)
    for g in range(o_ref.shape[0]):
        o_ref[g] = res

def combine(r, copies):
    B, _, D = r.shape
    return pl.pallas_call(
        combine_kernel,
        in_specs=[pl.BlockSpec(memory_space=pltpu.VMEM)],
        out_specs=pl.BlockSpec(memory_space=pltpu.VMEM),
        out_shape=jax.ShapeDtypeStruct((copies, 32, 2 * D), jnp.bfloat16),
        scratch_shapes=[pltpu.VMEM((B * 16, D), jnp.float32)],
        compiler_params=pltpu.CompilerParams(vmem_limit_bytes=10 << 20),
        cost_estimate=pl.CostEstimate(flops=1 << 20, bytes_accessed=1 << 20, transcendentals=0),
        name="combine",
    )(r)

def spread_kernel(q_ref, o_ref):
    M, HQ, D = o_ref.shape
    q = q_ref[...].astype(jnp.float32)
    x = jnp.concatenate([q[:, h * D:(h + 1) * D] for h in range(HQ)], axis=0).astype(jnp.bfloat16)
    for i in range(M):
        o_ref[i] = x

def spread(q, members, width):
    vm = pl.BlockSpec(memory_space=pltpu.VMEM)
    return pl.pallas_call(
        spread_kernel, in_specs=[vm], out_specs=vm,
        out_shape=jax.ShapeDtypeStruct((members, q.shape[1] // width, width), q.dtype),
        compiler_params=pltpu.CompilerParams(vmem_limit_bytes=10 << 20),
        cost_estimate=pl.CostEstimate(flops=1 << 18, bytes_accessed=1 << 19, transcendentals=0),
        name="spread",
    )(q)

def body(query, prompt_code_cache, prompt_scale_cache, prefix_len, sample_key_value_cache, suffix_len, w_out):
    chunk = prompt_code_cache.shape[1]
    head_width = prompt_code_cache.shape[3]
    members = lax.axis_size("prefix")
    groups = lax.axis_size("samples")
    me = lax.axis_index("prefix").astype(jnp.int32)
    valid = jnp.clip(prefix_len - me * chunk, 0, chunk)

    def swap(x, axis):
        return lax.all_to_all(x, axis, split_axis=0, concat_axis=0, tiled=True)

    gathered = swap(spread(query, members, head_width), "prefix")
    keys, values, own = prep(valid, suffix_len, prompt_scale_cache, prompt_code_cache, query, sample_key_value_cache)
    partials = attn(valid, me[None], gathered, keys, values, own)
    attention = combine(swap(partials, "prefix"), groups)
    rows = swap(attention, "samples").reshape(-1, attention.shape[2])
    terms = jnp.dot(rows, w_out, preferred_element_type=jnp.float32).astype(jnp.bfloat16)
    terms = swap(terms.reshape(members, -1, terms.shape[1]), "prefix")
    return jnp.sum(terms.astype(jnp.float32), axis=0).astype(jnp.bfloat16)


def solution(mesh):
    in_specs = (
        P(("samples", "prefix"), None),
        P(None, "prefix", None, None),
        P(None, "prefix", None),
        P(),
        P(("samples", "prefix"), None, None, None),
        P(("samples", "prefix")),
        P("prefix", "samples"),
    )
    return jax.shard_map(body, mesh=mesh, in_specs=in_specs, out_specs=P("prefix", "samples"), check_vma=False)
```

time: 110 us -> 99.4 us (0.904)
  local copies, waits for them, and re-layouts: 9.16 us -> 3.09 us
  waiting for transfers between devices: 0.01 us -> 4.32 us
  blocking collectives: 61.3 us -> 57.1 us
  Pallas kernels: 24.2 us -> 20.7 us
    unnamed x10 -> x6, local copies, waits for them, and re-layouts: 7.36 us -> 1.65 us
    all_to_all x1, waiting for transfers between devices: 0.01 us -> 4.32 us  [swap(): return lax.all_to_all(x, axis, split_axis=0, concat_axis=0, tiled=True)]
    all_to_all x3, blocking collectives: 61.3 us -> 57.1 us  [swap(): return lax.all_to_all(x, axis, split_axis=0, concat_axis=0, tiled=True)]
    pallas_call x3, Pallas kernels: 23.6 us -> 20.1 us  [the longest x1 10.1 us: prep(): pl.pallas_call(functools.partial(prep_kernel, tb=tb, sb=sb, cs=LOG2E / ma...]
  transfers between devices with their start and end apart: 1 -> 1, of which waited for: 0 -> 1; matrix products, arithmetic and copies ran while one was open for 1% -> 1% of each run, Pallas kernels for 10% -> 10%
where the time goes in v2:
time: 99.4 us; the launch traced here: 98.9 us
  blocking collectives  57.1 us (57%)
  Pallas kernels  20.7 us (21%)
  starting transfers between devices  11.4 us (11%)
  waiting for transfers between devices  4.32 us (4%)
  local copies, waits for them, and re-layouts  3.09 us (3%)
  between operations  1.35 us (1%)
    all_to_all x3, blocking collectives, swap(): return lax.all_to_all(x, axis, split_axis=0, concat_axis=0, tiled=True)  57.1 us
    all_to_all x1, starting transfers between devices, swap(): return lax.all_to_all(x, axis, split_axis=0, concat_axis=0, tiled=True)  11.4 us
    pallas_call x1, Pallas kernels, prep(): pl.pallas_call(functools.partial(prep_kernel, tb=tb, sb=sb, cs=LOG2E / ma...  10.1 us
    pallas_call x1, Pallas kernels, attn(): pl.pallas_call(functools.partial(attn_kernel, cs=LOG2E / math.sqrt(D), ti...  9.12 us
    all_to_all x1, waiting for transfers between devices, swap(): return lax.all_to_all(x, axis, split_axis=0, concat_axis=0, tiled=True)  4.32 us
  transfers between devices with their start and end apart: 1, of which 1 were waited for; matrix products, arithmetic and copies ran while one was open for 1% of the time, Pallas kernels for 10%

profile of v2, /device:TPU:32, one launch (start us, length us, event | category | flops | bytes accessed | tf_op | source)
XLA Modules:
  0.0 98.9 jit_solution(16830448025220404419)
XLA Ops:
  0.0 0.0 copy-start
  0.0 0.0 copy-start.1
  0.0 0.8 copy-done.1
  0.8 0.9 spread.1
  1.7 11.4 %all-to-all-start = ((bf16[32,64,128]{2,1,0:T(8,128)(2,1)}), bf16[32,64,128]{2,1,0:T(8,128)(2,1)S(1)}, u32[]{:S(2)}, u32[]{:S(2)}) async-start(bf16[32,64,128]{2,1,0:T(8,128)(2,1)} %spread.1), calls=%async_computation | async-start | bytes 1048576 | tf_op jit(solution)/shard_map/all_to_all | solution.py:311
  14.4 0.8 copy.9
  15.2 0.7 reshape.20.sc_ref
  15.8 10.1 %prep.1 = (bf16[8,2048,128]{2,1,0:T(8,128)(2,1)}, bf16[8,2048,128]{2,1,0:T(8,128)(2,1)}, f32[3,64,128]{2,1,0:T(8,128)}) custom-call(s32[1]{0:T(128)S(6)} %min.6.n_ref, s32[1]{0:T(128)S(6)} %copy.11.len_ref, f32[2,256]{1,0:T(2,128)} %reshape.20.sc_ref, bf16[2,16384,128]{2,1,0:T(8,128)(2,1)} %bitcast.8, bf16[1,8192]{1,0:T(2,128)(2,1)} %q_ref.3, ...), custom_call_target="tpu_custom_call" | custom-call | flops 16777216 | bytes 20971520 | tf_op jit(solution)/shard_map/prep/pallas_call | solution.py:124
  26.0 4.3 %all-to-all-done.qg_hbm = bf16[32,64,128]{2,1,0:T(8,128)(2,1)S(1)} async-done(((bf16[32,64,128]{2,1,0:T(8,128)(2,1)}), bf16[32,64,128]{2,1,0:T(8,128)(2,1)S(1)}, u32[]{:S(2)}, u32[]{:S(2)}) %all-to-all-start) | async-done | bytes 524320 | tf_op jit(solution)/shard_map/all_to_all | solution.py:311
  30.3 0.0 copy-start.2
  30.3 0.8 copy-done.2
  31.1 9.1 %attn.1 = bf16[32,80,128]{2,1,0:T(8,128)(2,1)} custom-call(s32[1]{0:T(128)S(6)} %min.6.n_ref, s32[1]{0:T(128)} %bitcast.1.me_ref, bf16[32,64,128]{2,1,0:T(8,128)(2,1)} %copy-done.2, bf16[8,2048,128]{2,1,0:T(8,128)(2,1)} %get-tuple-element.8.k_hbm, bf16[8,2048,128]{2,1,0:T(8,128)(2,1)} %get-tuple-element.9.v_hbm, f32[3,64,128]{2,1,0:T(8,128)} %get-tuple-element.10.own_hbm), custom_call_target="tpu_custom_call" | custom-call | flops 2147483648 | bytes 12582912 | tf_op jit(solution)/shard_map/attn/pallas_call | solution.py:241
  40.2 24.6 %all_to_all.20.r_ref = bf16[32,80,128]{2,1,0:T(8,128)(2,1)S(1)} all-to-all(bf16[32,80,128]{2,1,0:T(8,128)(2,1)} %attn.1), channel_id=1, replica_groups=mesh['prefix'=32,'samples'=8] {'prefix'}, dimensions={0} | all-to-all | bytes 1310720 | tf_op jit(solution)/shard_map/all_to_all | solution.py:311
  64.9 0.6 combine.1
  65.4 10.2 %all_to_all.21 = bf16[8,32,256]{2,1,0:T(8,128)(2,1)S(1)} all-to-all(bf16[8,32,256]{2,1,0:T(8,128)(2,1)S(1)} %combine.1), channel_id=1, replica_groups=mesh['prefix'=32,'samples'=8] {'samples'}, dimensions={0} | all-to-all | bytes 262144 | tf_op jit(solution)/shard_map/all_to_all | solution.py:311
  75.7 0.0 copy-done
  75.7 0.3 fusion
  76.0 22.2 %all_to_all.22 = bf16[32,8,1024]{2,1,0:T(8,128)(2,1)S(1)} all-to-all(bf16[32,8,1024]{2,1,0:T(8,128)(2,1)S(1)} %fusion), channel_id=1, replica_groups=mesh['prefix'=32,'samples'=8] {'prefix'}, dimensions={0} | all-to-all | bytes 1048576 | tf_op jit(solution)/shard_map/all_to_all | solution.py:311
  98.2 0.7 reduce_sum.12
Async XLA Ops:
  0.0 75.7 %copy-start = (bf16[256,1024]{1,0:T(8,128)(2,1)S(1)}, bf16[256,1024]{1,0:T(8,128)(2,1)}, u32[]{:S(2)}) copy-start(bf16[256,1024]{1,0:T(8,128)(2,1)} %param.13) | copy-start | bytes 1572868
  0.0 0.8 copy-start.1
  1.7 28.6 %all-to-all-start = ((bf16[32,64,128]{2,1,0:T(8,128)(2,1)}), bf16[32,64,128]{2,1,0:T(8,128)(2,1)S(1)}, u32[]{:S(2)}, u32[]{:S(2)}) async-start(bf16[32,64,128]{2,1,0:T(8,128)(2,1)} %spread.1), calls=%async_computation | async-start | bytes 1048576 | tf_op jit(solution)/shard_map/all_to_all | solution.py:311
  30.3 0.8 copy-start.2

commit v3 on v2

--- a/solution.py
+++ b/solution.py
@@ -7,8 +7,11 @@
 LOG2E = 1.4426950408889634
 FLOOR = -(2.0 ** 127)
 
-def prep_kernel(n_ref, len_ref, sc_ref, code_hbm, q_ref, cache_hbm, k_hbm, v_hbm, own_ref, code_s, cache_s, k_s, v_s, hot_s, in_sem, cache_sem, k_sem, v_sem, *, tb, sb, cs):
-    H, _, lanes = k_s.shape
+def valid_rows(plen_ref, chunk):
+    return jnp.clip(plen_ref[0] - lax.axis_index("prefix") * chunk, 0, chunk)
+
+def prep_kernel(plen_ref, len_ref, scale_ref, code_hbm, q_ref, cache_hbm, k_hbm, v_hbm, own_ref, code_s, cache_s, k_s, v_s, hot_s, sc_v, sc_ref, sc_sem, in_sem, cache_sem, k_sem, v_sem, *, tb, sb, cs):
+    H, T, lanes = k_s.shape
     G = own_ref.shape[1] // H
     steps = k_s.shape[1] // tb
 
@@ -28,16 +31,24 @@
     cache_copy.start()
     for i in range(1, steps):
         load(i).start()
+    B = scale_ref.shape[2]
+    for c in range(2):
+        sc_v[c * H:(c + 1) * H, 0:B] = scale_ref[c].astype(jnp.float32)
+    sc_copy = pltpu.make_async_copy(sc_v, sc_ref, sc_sem)
+    sc_copy.start()
+    n = valid_rows(plen_ref, T)
     hr = hot_s.shape[0]
     half = sb // 2
     r = lax.broadcasted_iota(jnp.int32, (hr, hr), 0)
     c = lax.broadcasted_iota(jnp.int32, (hr, hr), 1)
     hot_s[...] = jnp.where((r % half) * H + r // half == c, 1.0, 0.0).astype(jnp.bfloat16)
 
+    sc_copy.wait()
+
     @pl.loop(0, steps)
     def _(i):
         load(i).wait()
-        prep_step(i, n_ref, sc_ref, code_s, k_s, v_s, hot_s, tb=tb, sb=sb)
+        prep_step(i, n, sc_ref, code_s, k_s, v_s, hot_s, tb=tb, sb=sb)
         for copy in save(i):
             copy.start()
 
@@ -47,9 +58,9 @@
         own = jnp.concatenate([q[:, h * lanes:(h + 1) * lanes] for h in range(i * G, (i + 1) * G)], axis=0).astype(jnp.bfloat16)
         cols = slice(i * lanes, (i + 1) * lanes)
         grp = slice(i * G, (i + 1) * G)
-        T = cache_s.shape[2]
+        C = cache_s.shape[2]
         s = lax.dot_general(own, cache_s[0, 0, :, cols], (((1,), (1,)), ((), ())), preferred_element_type=jnp.float32) * cs
-        s = jnp.where(lax.broadcasted_iota(jnp.int32, (G, T), 1) < len_ref[0], s, -jnp.inf)
+        s = jnp.where(lax.broadcasted_iota(jnp.int32, (G, C), 1) < len_ref[0], s, -jnp.inf)
         m = jnp.max(s, axis=1, keepdims=True)
         w = jnp.exp2(s - m).astype(jnp.bfloat16)
         own_ref[0, grp, :] = jnp.dot(w, cache_s[0, 1, :, cols], preferred_element_type=jnp.float32)
@@ -60,18 +71,17 @@
             copy.wait()
 
 
-def prep_step(i, n_ref, sc_ref, code_ref, k_ref, v_ref, hot_s, *, tb, sb):
+def prep_step(i, n, sc_ref, code_ref, k_ref, v_ref, hot_s, *, tb, sb):
     heads = k_ref.shape[0]
     lanes = code_ref.shape[2]
     half = sb // 2
     hr = half * heads
-    n = n_ref[0]
 
     def move(c, b):
         x = jnp.concatenate([code_ref[c, pl.ds(pl.multiple_of(i * tb * heads, tb * heads) + (2 * b + u) * hr, hr), :] for u in range(2)], axis=1)
         y = jnp.dot(hot_s[...], x, preferred_element_type=jnp.float32)
         blk = i * (tb // sb) + b
-        return [y[j * half:(j + 1) * half] * sc_ref[c, blk * heads + j] for j in range(heads)]
+        return [y[j * half:(j + 1) * half] * sc_ref[c * heads + j, blk] for j in range(heads)]
 
     def go(masked):
         for b in range(tb // sb):
@@ -114,34 +124,34 @@
 
 def prep(n, length, scale, code, q, cache):
     _, T, H, D = code.shape
-    tb = T // 4
+    tb = T // 8
     sb = T // scale.shape[1]
     G = q.shape[1] // (H * D)
-    sc = scale.astype(jnp.float32).reshape(2, -1)
     smem = pl.BlockSpec(memory_space=pltpu.SMEM)
     vmem = pl.BlockSpec(memory_space=pltpu.VMEM)
     hbm = pl.BlockSpec(memory_space=pltpu.HBM)
     return pl.pallas_call(
         functools.partial(prep_kernel, tb=tb, sb=sb, cs=LOG2E / math.sqrt(D)),
-        in_specs=[smem, smem, smem, hbm, vmem, hbm],
+        in_specs=[smem, smem, vmem, hbm, vmem, hbm],
         out_specs=[hbm, hbm, vmem],
         out_shape=[jax.ShapeDtypeStruct((H, T, D), jnp.bfloat16)] * 2 + [jax.ShapeDtypeStruct((3, H * G, D), jnp.float32)],
         scratch_shapes=[pltpu.VMEM((2, T * H, D), jnp.bfloat16), pltpu.VMEM(cache.shape, jnp.bfloat16),
                         pltpu.VMEM((H, T, D), jnp.bfloat16), pltpu.VMEM((H, T, D), jnp.bfloat16),
                         pltpu.VMEM((sb // 2 * H, sb // 2 * H), jnp.bfloat16),
+                        pltpu.VMEM((2 * H, 128), jnp.float32), pltpu.SMEM((2 * H, 128), jnp.float32), pltpu.SemaphoreType.DMA,
                         pltpu.SemaphoreType.DMA((T // tb,)), pltpu.SemaphoreType.DMA,
                         pltpu.SemaphoreType.DMA((T // tb,)), pltpu.SemaphoreType.DMA((T // tb,))],
         compiler_params=pltpu.CompilerParams(vmem_limit_bytes=63_300_000),
         cost_estimate=pl.CostEstimate(flops=16 << 20, bytes_accessed=20 << 20, transcendentals=0),
         name="prep",
-    )(n, length, sc, code.reshape(2, T * H, D), q, cache)
-
-def attn_kernel(n_ref, me_ref, qg_hbm, k_hbm, v_hbm, own_hbm, out_ref, qg_ref, own_ref, qg_sem, own_sem, q_s, k_ref, v_ref, one_s, k_sem, v_sem, *s_s, cs, tile, nbuf):
+    )(n, length, scale.transpose(0, 2, 1), code.reshape(2, T * H, D), q, cache)
+
+def attn_kernel(plen_ref, qg_hbm, k_hbm, v_hbm, own_hbm, out_ref, qg_ref, own_ref, qg_sem, own_sem, q_s, k_ref, v_ref, one_s, k_sem, v_sem, *s_s, cs, tile, nbuf):
     S, HQ, D = qg_ref.shape
     H, T, _ = k_hbm.shape
     G = HQ // H
-    n = n_ref[0]
-    me = me_ref[0]
+    n = valid_rows(plen_ref, T)
+    me = lax.axis_index("prefix")
     R = G * S
     hp = 64 // S
     load_k = [pltpu.make_async_copy(k_hbm.at[j], k_ref.at[j], k_sem.at[j]) for j in range(H)]
@@ -206,8 +216,8 @@
             mr = jnp.sum(jnp.where(diag, mm, 0.0), axis=0, keepdims=True)
             tr = jnp.sum(jnp.where(diag, tt, 0.0), axis=0, keepdims=True)
             hi = tr.astype(jnp.bfloat16).astype(jnp.float32)
-            st = jnp.concatenate([mr, hi, tr - hi, jnp.zeros((13, D), jnp.float32)], axis=0)
-            out_ref[j * (G // hp) + d0, 64:80, :] = st.astype(jnp.bfloat16)
+            st = jnp.concatenate([mr, hi, tr - hi, jnp.zeros((5, D), jnp.float32)], axis=0)
+            out_ref[j * (G // hp) + d0, 64:72, :] = st.astype(jnp.bfloat16)
     nt = T // tile
     K = lambda *a: [('k', i) for i in a]
     V = lambda *a: [('v', i) for i in a]
@@ -232,7 +242,7 @@
         if j > 0:
             finish(j - 1)
 
-def attn(n, me, qg, k, v, own, tile=256, nbuf=2):
+def attn(n, qg, k, v, own, tile=256, nbuf=2):
     S, HQ, D = qg.shape
     H, T, _ = k.shape
     nd = HQ * S // 64
@@ -240,22 +250,22 @@
     hbm = pl.BlockSpec(memory_space=pltpu.HBM)
     return pl.pallas_call(
         functools.partial(attn_kernel, cs=LOG2E / math.sqrt(D), tile=tile, nbuf=nbuf),
-        in_specs=[pl.BlockSpec(memory_space=pltpu.SMEM)] * 2 + [hbm] * 4,
+        in_specs=[pl.BlockSpec(memory_space=pltpu.SMEM)] + [hbm] * 4,
         out_specs=vm,
-        out_shape=jax.ShapeDtypeStruct((nd, 80, D), jnp.bfloat16),
+        out_shape=jax.ShapeDtypeStruct((nd, 72, D), jnp.bfloat16),
         scratch_shapes=[pltpu.VMEM(qg.shape, qg.dtype), pltpu.VMEM(own.shape, own.dtype), pltpu.SemaphoreType.DMA, pltpu.SemaphoreType.DMA, pltpu.VMEM((S * HQ, D), jnp.float32), pltpu.VMEM((H, T, D), jnp.bfloat16), pltpu.VMEM((H, T, D), jnp.bfloat16), pltpu.VMEM((T, D), jnp.bfloat16),
                         pltpu.SemaphoreType.DMA((H,)), pltpu.SemaphoreType.DMA((H,))] + [pltpu.VMEM((S * HQ // H, T), jnp.float32)] * nbuf,
         compiler_params=pltpu.CompilerParams(vmem_limit_bytes=63_300_000),
         cost_estimate=pl.CostEstimate(flops=2 << 30, bytes_accessed=12 << 20, transcendentals=4 << 20),
         name="attn",
-    )(n, me, qg, k, v, own)
+    )(n, qg, k, v, own)
 
 def combine_kernel(r_ref, o_ref, st_s):
     B = r_ref.shape[0]
     D = r_ref.shape[2]
-    st_s[...] = r_ref[:, 64:80, :].astype(jnp.float32).reshape(B * 16, D)
-    m = st_s[pl.ds(0, B, stride=16), :]
-    t = st_s[pl.ds(1, B, stride=16), :] + st_s[pl.ds(2, B, stride=16), :]
+    st_s[...] = r_ref[:, 64:72, :].astype(jnp.float32).reshape(B * 8, D)
+    m = st_s[pl.ds(0, B, stride=8), :]
+    t = st_s[pl.ds(1, B, stride=8), :] + st_s[pl.ds(2, B, stride=8), :]
     M = jnp.max(m, axis=0, keepdims=True)
     f = jnp.exp2(m - M)
     den = jnp.sum(f * t, axis=0, keepdims=True)
@@ -276,7 +286,7 @@
         in_specs=[pl.BlockSpec(memory_space=pltpu.VMEM)],
         out_specs=pl.BlockSpec(memory_space=pltpu.VMEM),
         out_shape=jax.ShapeDtypeStruct((copies, 32, 2 * D), jnp.bfloat16),
-        scratch_shapes=[pltpu.VMEM((B * 16, D), jnp.float32)],
+        scratch_shapes=[pltpu.VMEM((B * 8, D), jnp.float32)],
         compiler_params=pltpu.CompilerParams(vmem_limit_bytes=10 << 20),
         cost_estimate=pl.CostEstimate(flops=1 << 20, bytes_accessed=1 << 20, transcendentals=0),
         name="combine",
@@ -300,19 +310,16 @@
     )(q)
 
 def body(query, prompt_code_cache, prompt_scale_cache, prefix_len, sample_key_value_cache, suffix_len, w_out):
-    chunk = prompt_code_cache.shape[1]
     head_width = prompt_code_cache.shape[3]
     members = lax.axis_size("prefix")
     groups = lax.axis_size("samples")
-    me = lax.axis_index("prefix").astype(jnp.int32)
-    valid = jnp.clip(prefix_len - me * chunk, 0, chunk)
 
     def swap(x, axis):
         return lax.all_to_all(x, axis, split_axis=0, concat_axis=0, tiled=True)
 
     gathered = swap(spread(query, members, head_width), "prefix")
-    keys, values, own = prep(valid, suffix_len, prompt_scale_cache, prompt_code_cache, query, sample_key_value_cache)
-    partials = attn(valid, me[None], gathered, keys, values, own)
+    keys, values, own = prep(prefix_len, suffix_len, prompt_scale_cache, prompt_code_cache, query, sample_key_value_cache)
+    partials = attn(prefix_len, gathered, keys, values, own)
     attention = combine(swap(partials, "prefix"), groups)
     rows = swap(attention, "samples").reshape(-1, attention.shape[2])
     terms = jnp.dot(rows, w_out, preferred_element_type=jnp.float32).astype(jnp.bfloat16)

time: 99.4 us -> 97.4 us (0.980)
  blocking collectives: 57.1 us -> 55.1 us
  local copies, waits for them, and re-layouts: 3.09 us -> 1.65 us
    all_to_all x3, blocking collectives: 57.1 us -> 55.1 us  [swap(): return lax.all_to_all(x, axis, split_axis=0, concat_axis=0, tiled=True)]
    reshape x2 -> x0, local copies, waits for them, and re-layouts: 1.44 us -> none  [prep(): sc = scale.astype(jnp.float32).reshape(2, -1)]
  transfers between devices with their start and end apart: 1 -> 1, of which waited for: 1 -> 1; matrix products, arithmetic and copies ran while one was open for 1% -> 0% of each run, Pallas kernels for 10% -> 11%
where the time goes in v3:
time: 97.4 us; the launch traced here: 96.9 us
  blocking collectives  55.1 us (57%)
  Pallas kernels  21.2 us (22%)
  starting transfers between devices  11.4 us (12%)
  waiting for transfers between devices  5.21 us (5%)
  local copies, waits for them, and re-layouts  1.65 us (2%)
  between operations  1.34 us (1%)
    all_to_all x3, blocking collectives, swap(): return lax.all_to_all(x, axis, split_axis=0, concat_axis=0, tiled=True)  55.1 us
    all_to_all x1, starting transfers between devices, swap(): return lax.all_to_all(x, axis, split_axis=0, concat_axis=0, tiled=True)  11.4 us
    pallas_call x1, Pallas kernels, prep(): pl.pallas_call(functools.partial(prep_kernel, tb=tb, sb=sb, cs=LOG2E / ma...  10.7 us
    pallas_call x1, Pallas kernels, attn(): pl.pallas_call(functools.partial(attn_kernel, cs=LOG2E / math.sqrt(D), ti...  9.09 us
    all_to_all x1, waiting for transfers between devices, swap(): return lax.all_to_all(x, axis, split_axis=0, concat_axis=0, tiled=True)  5.21 us
  transfers between devices with their start and end apart: 1, of which 1 were waited for; matrix products, arithmetic and copies ran while one was open for 0% of the time, Pallas kernels for 11%

profile of v3, /device:TPU:32, one launch (start us, length us, event | category | flops | bytes accessed | tf_op | source)
XLA Modules:
  0.0 96.9 jit_solution(6111703083092175327)
XLA Ops:
  0.0 0.0 copy-start
  0.0 0.0 copy-start.1
  0.0 0.8 copy-done.1
  0.8 0.9 spread.1
  1.7 11.4 %all-to-all-start = ((bf16[32,64,128]{2,1,0:T(8,128)(2,1)}), bf16[32,64,128]{2,1,0:T(8,128)(2,1)S(1)}, u32[]{:S(2)}, u32[]{:S(2)}) async-start(bf16[32,64,128]{2,1,0:T(8,128)(2,1)} %spread.1), calls=%async_computation | async-start | bytes 1048576 | tf_op jit(solution)/shard_map/all_to_all | solution.py:318
  14.4 10.7 %prep.1 = (bf16[8,2048,128]{2,1,0:T(8,128)(2,1)}, bf16[8,2048,128]{2,1,0:T(8,128)(2,1)}, f32[3,64,128]{2,1,0:T(8,128)}) custom-call(s32[1]{0:T(128)S(6)} %copy.8.plen_ref, s32[1]{0:T(128)S(6)} %copy.9.len_ref, bf16[2,8,32]{2,1,0:T(8,128)(2,1)} %bitcast.9, bf16[2,16384,128]{2,1,0:T(8,128)(2,1)} %bitcast.7, bf16[1,8192]{1,0:T(2,128)(2,1)} %q_ref.3, ...), custom_call_target="tpu_custom_call" | custom-call | flops 16777216 | bytes 20971520 | tf_op jit(solution)/shard_map/prep/pallas_call | solution.py:133
  25.1 5.2 %all-to-all-done.qg_hbm = bf16[32,64,128]{2,1,0:T(8,128)(2,1)S(1)} async-done(((bf16[32,64,128]{2,1,0:T(8,128)(2,1)}), bf16[32,64,128]{2,1,0:T(8,128)(2,1)S(1)}, u32[]{:S(2)}, u32[]{:S(2)}) %all-to-all-start) | async-done | bytes 524320 | tf_op jit(solution)/shard_map/all_to_all | solution.py:318
  30.3 0.0 copy-start.2
  30.3 0.8 copy-done.2
  31.1 9.1 %attn.1 = bf16[32,72,128]{2,1,0:T(8,128)(2,1)} custom-call(s32[1]{0:T(128)S(6)} %copy.8.plen_ref, bf16[32,64,128]{2,1,0:T(8,128)(2,1)} %copy-done.2, bf16[8,2048,128]{2,1,0:T(8,128)(2,1)} %get-tuple-element.8.k_hbm, bf16[8,2048,128]{2,1,0:T(8,128)(2,1)} %get-tuple-element.9.v_hbm, f32[3,64,128]{2,1,0:T(8,128)} %get-tuple-element.10.own_hbm), custom_call_target="tpu_custom_call" | custom-call | flops 2147483648 | bytes 12582912 | tf_op jit(solution)/shard_map/attn/pallas_call | solution.py:251
  40.2 22.9 %all_to_all.20.r_ref = bf16[32,72,128]{2,1,0:T(8,128)(2,1)S(1)} all-to-all(bf16[32,72,128]{2,1,0:T(8,128)(2,1)} %attn.1), channel_id=1, replica_groups=mesh['prefix'=32,'samples'=8] {'prefix'}, dimensions={0} | all-to-all | bytes 1179648 | tf_op jit(solution)/shard_map/all_to_all | solution.py:318
  63.1 0.5 combine.1
  63.6 10.2 %all_to_all.21 = bf16[8,32,256]{2,1,0:T(8,128)(2,1)S(1)} all-to-all(bf16[8,32,256]{2,1,0:T(8,128)(2,1)S(1)} %combine.1), channel_id=1, replica_groups=mesh['prefix'=32,'samples'=8] {'samples'}, dimensions={0} | all-to-all | bytes 262144 | tf_op jit(solution)/shard_map/all_to_all | solution.py:318
  73.9 0.0 copy-done
  73.9 0.3 fusion
  74.2 22.1 %all_to_all.22 = bf16[32,8,1024]{2,1,0:T(8,128)(2,1)S(1)} all-to-all(bf16[32,8,1024]{2,1,0:T(8,128)(2,1)S(1)} %fusion), channel_id=1, replica_groups=mesh['prefix'=32,'samples'=8] {'prefix'}, dimensions={0} | all-to-all | bytes 1048576 | tf_op jit(solution)/shard_map/all_to_all | solution.py:318
  96.2 0.7 reduce_sum.12
Async XLA Ops:
  0.0 73.9 %copy-start = (bf16[256,1024]{1,0:T(8,128)(2,1)S(1)}, bf16[256,1024]{1,0:T(8,128)(2,1)}, u32[]{:S(2)}) copy-start(bf16[256,1024]{1,0:T(8,128)(2,1)} %param.13) | copy-start | bytes 1572868
  0.0 0.8 copy-start.1
  1.7 28.6 %all-to-all-start = ((bf16[32,64,128]{2,1,0:T(8,128)(2,1)}), bf16[32,64,128]{2,1,0:T(8,128)(2,1)S(1)}, u32[]{:S(2)}, u32[]{:S(2)}) async-start(bf16[32,64,128]{2,1,0:T(8,128)(2,1)} %spread.1), calls=%async_computation | async-start | bytes 1048576 | tf_op jit(solution)/shard_map/all_to_all | solution.py:318
  30.3 0.8 copy-start.2

commit v4 on v3

--- a/solution.py
+++ b/solution.py
@@ -10,7 +10,7 @@
 def valid_rows(plen_ref, chunk):
     return jnp.clip(plen_ref[0] - lax.axis_index("prefix") * chunk, 0, chunk)
 
-def prep_kernel(plen_ref, len_ref, scale_ref, code_hbm, q_ref, cache_hbm, k_hbm, v_hbm, own_ref, code_s, cache_s, k_s, v_s, hot_s, sc_v, sc_ref, sc_sem, in_sem, cache_sem, k_sem, v_sem, *, tb, sb, cs):
+def prep_kernel(plen_ref, len_ref, scale_ref, code_hbm, q_ref, cache_hbm, kv_hbm, own_hbm, own_ref, own_sem, code_s, cache_s, k_s, v_s, hot_s, sc_v, sc_ref, sc_sem, in_sem, cache_sem, k_sem, v_sem, *, tb, sb, cs):
     H, T, lanes = k_s.shape
     G = own_ref.shape[1] // H
     steps = k_s.shape[1] // tb
@@ -23,8 +23,8 @@
 
     def save(i):
         at = rows(i, tb)
-        return (pltpu.make_async_copy(k_s.at[:, at, :], k_hbm.at[:, at, :], k_sem.at[i]),
-                pltpu.make_async_copy(v_s.at[:, at, :], v_hbm.at[:, at, :], v_sem.at[i]))
+        return (pltpu.make_async_copy(k_s.at[:, at, :], kv_hbm.at[0, :, at, :], k_sem.at[i]),
+                pltpu.make_async_copy(v_s.at[:, at, :], kv_hbm.at[1, :, at, :], v_sem.at[i]))
 
     cache_copy = pltpu.make_async_copy(cache_hbm, cache_s, cache_sem)
     load(0).start()
@@ -66,9 +66,12 @@
         own_ref[0, grp, :] = jnp.dot(w, cache_s[0, 1, :, cols], preferred_element_type=jnp.float32)
         own_ref[1, grp, :] = jnp.broadcast_to(m, (G, lanes))
         own_ref[2, grp, :] = jnp.broadcast_to(jnp.sum(w.astype(jnp.float32), axis=1, keepdims=True), (G, lanes))
+    own_copy = pltpu.make_async_copy(own_ref, own_hbm.at[0:3], own_sem)
+    own_copy.start()
     for i in range(steps):
         for copy in save(i):
             copy.wait()
+    own_copy.wait()
 
 
 def prep_step(i, n, sc_ref, code_ref, k_ref, v_ref, hot_s, *, tb, sb):
@@ -133,9 +136,9 @@
     return pl.pallas_call(
         functools.partial(prep_kernel, tb=tb, sb=sb, cs=LOG2E / math.sqrt(D)),
         in_specs=[smem, smem, vmem, hbm, vmem, hbm],
-        out_specs=[hbm, hbm, vmem],
-        out_shape=[jax.ShapeDtypeStruct((H, T, D), jnp.bfloat16)] * 2 + [jax.ShapeDtypeStruct((3, H * G, D), jnp.float32)],
-        scratch_shapes=[pltpu.VMEM((2, T * H, D), jnp.bfloat16), pltpu.VMEM(cache.shape, jnp.bfloat16),
+        out_specs=[hbm, hbm],
+        out_shape=[jax.ShapeDtypeStruct((4, H, T, D), jnp.bfloat16)] + [jax.ShapeDtypeStruct((480, H * G, D), jnp.float32)],
+        scratch_shapes=[pltpu.VMEM((3, H * G, D), jnp.float32), pltpu.SemaphoreType.DMA, pltpu.VMEM((2, T * H, D), jnp.bfloat16), pltpu.VMEM(cache.shape, jnp.bfloat16),
                         pltpu.VMEM((H, T, D), jnp.bfloat16), pltpu.VMEM((H, T, D), jnp.bfloat16),
                         pltpu.VMEM((sb // 2 * H, sb // 2 * H), jnp.bfloat16),
                         pltpu.VMEM((2 * H, 128), jnp.float32), pltpu.SMEM((2 * H, 128), jnp.float32), pltpu.SemaphoreType.DMA,
@@ -146,26 +149,23 @@
         name="prep",
     )(n, length, scale.transpose(0, 2, 1), code.reshape(2, T * H, D), q, cache)
 
-def attn_kernel(plen_ref, qg_hbm, k_hbm, v_hbm, own_hbm, out_ref, qg_ref, own_ref, qg_sem, own_sem, q_s, k_ref, v_ref, one_s, k_sem, v_sem, *s_s, cs, tile, nbuf):
+def attn_kernel(plen_ref, qg_ref, kv_hbm, own_hbm, out_ref, own_ref, own_sem, q_s, k_ref, v_ref, one_s, k_sem, v_sem, *s_s, cs, tile, nbuf):
     S, HQ, D = qg_ref.shape
-    H, T, _ = k_hbm.shape
+    _, H, T, _ = kv_hbm.shape
     G = HQ // H
     n = valid_rows(plen_ref, T)
     me = lax.axis_index("prefix")
     R = G * S
     hp = 64 // S
-    load_k = [pltpu.make_async_copy(k_hbm.at[j], k_ref.at[j], k_sem.at[j]) for j in range(H)]
-    load_v = [pltpu.make_async_copy(v_hbm.at[j], v_ref.at[j], v_sem.at[j]) for j in range(H)]
-    load_own = pltpu.make_async_copy(own_hbm, own_ref, own_sem)
-    load_q = pltpu.make_async_copy(qg_hbm, qg_ref, qg_sem)
-    load_q.start()
+    load_k = [pltpu.make_async_copy(kv_hbm.at[0, j], k_ref.at[j], k_sem.at[j]) for j in range(H)]
+    load_v = [pltpu.make_async_copy(kv_hbm.at[1, j], v_ref.at[j], v_sem.at[j]) for j in range(H)]
+    load_own = pltpu.make_async_copy(own_hbm.at[0:3], own_ref, own_sem)
     load_k[0].start()
     load_k[1].start()
     load_v[0].start()
     load_own.start()
     one_s[...] = jnp.where(lax.broadcasted_iota(jnp.int32, (T, D), 0) < n, 1.0, 0.0).astype(jnp.bfloat16)
     sidx = lax.broadcasted_iota(jnp.int32, (S, D), 0)
-    load_q.wait()
     q_s[...] = qg_ref[...].astype(jnp.float32).reshape(S * HQ, D)
     ms = {}
     def scores(j, c):
@@ -242,23 +242,23 @@
         if j > 0:
             finish(j - 1)
 
-def attn(n, qg, k, v, own, tile=256, nbuf=2):
+def attn(n, qg, kv, own, tile=256, nbuf=2):
     S, HQ, D = qg.shape
-    H, T, _ = k.shape
+    _, H, T, _ = kv.shape
     nd = HQ * S // 64
     vm = pl.BlockSpec(memory_space=pltpu.VMEM)
     hbm = pl.BlockSpec(memory_space=pltpu.HBM)
     return pl.pallas_call(
         functools.partial(attn_kernel, cs=LOG2E / math.sqrt(D), tile=tile, nbuf=nbuf),
-        in_specs=[pl.BlockSpec(memory_space=pltpu.SMEM)] + [hbm] * 4,
+        in_specs=[pl.BlockSpec(memory_space=pltpu.SMEM), vm, hbm, hbm],
         out_specs=vm,
         out_shape=jax.ShapeDtypeStruct((nd, 72, D), jnp.bfloat16),
-        scratch_shapes=[pltpu.VMEM(qg.shape, qg.dtype), pltpu.VMEM(own.shape, own.dtype), pltpu.SemaphoreType.DMA, pltpu.SemaphoreType.DMA, pltpu.VMEM((S * HQ, D), jnp.float32), pltpu.VMEM((H, T, D), jnp.bfloat16), pltpu.VMEM((H, T, D), jnp.bfloat16), pltpu.VMEM((T, D), jnp.bfloat16),
+        scratch_shapes=[pltpu.VMEM((3,) + own.shape[1:], own.dtype), pltpu.SemaphoreType.DMA, pltpu.VMEM((S * HQ, D), jnp.float32), pltpu.VMEM((H, T, D), jnp.bfloat16), pltpu.VMEM((H, T, D), jnp.bfloat16), pltpu.VMEM((T, D), jnp.bfloat16),
                         pltpu.SemaphoreType.DMA((H,)), pltpu.SemaphoreType.DMA((H,))] + [pltpu.VMEM((S * HQ // H, T), jnp.float32)] * nbuf,
-        compiler_params=pltpu.CompilerParams(vmem_limit_bytes=63_300_000),
+        compiler_params=pltpu.CompilerParams(vmem_limit_bytes=48_000_000),
         cost_estimate=pl.CostEstimate(flops=2 << 30, bytes_accessed=12 << 20, transcendentals=4 << 20),
         name="attn",
-    )(n, qg, k, v, own)
+    )(n, qg, kv, own)
 
 def combine_kernel(r_ref, o_ref, st_s):
     B = r_ref.shape[0]
@@ -318,8 +318,8 @@
         return lax.all_to_all(x, axis, split_axis=0, concat_axis=0, tiled=True)
 
     gathered = swap(spread(query, members, head_width), "prefix")
-    keys, values, own = prep(prefix_len, suffix_len, prompt_scale_cache, prompt_code_cache, query, sample_key_value_cache)
-    partials = attn(prefix_len, gathered, keys, values, own)
+    keys_values, own = prep(prefix_len, suffix_len, prompt_scale_cache, prompt_code_cache, query, sample_key_value_cache)
+    partials = attn(prefix_len, gathered, keys_values, own)
     attention = combine(swap(partials, "prefix"), groups)
     rows = swap(attention, "samples").reshape(-1, attention.shape[2])
     terms = jnp.dot(rows, w_out, preferred_element_type=jnp.float32).astype(jnp.bfloat16)

time: 97.4 us -> 95.1 us (0.976)
  Pallas kernels: 21.2 us -> 20.1 us
    pallas_call x1, Pallas kernels: 9.09 us -> 8.01 us  [attn(): pl.pallas_call(functools.partial(attn_kernel, cs=LOG2E / math.sqrt(D), ti...]
where the time goes in v4:
time: 95.1 us; the launch traced here: 94.7 us
  blocking collectives  54.9 us (58%)
  Pallas kernels  20.1 us (21%)
  starting transfers between devices  11.4 us (12%)
  waiting for transfers between devices  5.21 us (5%)
  between operations  1.34 us (1%)
    all_to_all x3, blocking collectives, swap(): return lax.all_to_all(x, axis, split_axis=0, concat_axis=0, tiled=True)  54.9 us
    all_to_all x1, starting transfers between devices, swap(): return lax.all_to_all(x, axis, split_axis=0, concat_axis=0, tiled=True)  11.4 us
    pallas_call x1, Pallas kernels, prep(): pl.pallas_call(functools.partial(prep_kernel, tb=tb, sb=sb, cs=LOG2E / ma...  10.7 us
    pallas_call x1, Pallas kernels, attn(): pl.pallas_call(functools.partial(attn_kernel, cs=LOG2E / math.sqrt(D), ti...  8.01 us
    all_to_all x1, waiting for transfers between devices, swap(): return lax.all_to_all(x, axis, split_axis=0, concat_axis=0, tiled=True)  5.21 us
  transfers between devices with their start and end apart: 1, of which 1 were waited for; matrix products, arithmetic and copies ran while one was open for 0% of the time, Pallas kernels for 11%

profile of v4, /device:TPU:32, one launch (start us, length us, event | category | flops | bytes accessed | tf_op | source)
XLA Modules:
  0.0 94.7 jit_solution(5060816701420457880)
XLA Ops:
  0.0 0.0 copy-start
  0.0 0.0 copy-start.1
  0.0 0.8 copy-done.1
  0.8 0.9 spread.1
  1.7 11.4 %all-to-all-start = ((bf16[32,64,128]{2,1,0:T(8,128)(2,1)}), bf16[32,64,128]{2,1,0:T(8,128)(2,1)S(1)}, u32[]{:S(2)}, u32[]{:S(2)}) async-start(bf16[32,64,128]{2,1,0:T(8,128)(2,1)} %spread.1), calls=%async_computation | async-start | bytes 1048576 | tf_op jit(solution)/shard_map/all_to_all | solution.py:318
  14.3 10.7 %prep.1 = (bf16[4,8,2048,128]{3,2,1,0:T(8,128)(2,1)}, f32[480,64,128]{2,1,0:T(8,128)}) custom-call(s32[1]{0:T(128)S(6)} %copy.8.plen_ref, s32[1]{0:T(128)S(6)} %copy.9.len_ref, bf16[2,8,32]{2,1,0:T(8,128)(2,1)} %bitcast.9, bf16[2,16384,128]{2,1,0:T(8,128)(2,1)} %bitcast.7, bf16[1,8192]{1,0:T(2,128)(2,1)} %q_ref.3, bf16[1,2,512,1024]{3,2,1,0:T(8,128)(2,1)} %cache_hbm.1), custom_call_target="tpu_custom_call" | custom-call | flops 16777216 | bytes 20971520 | tf_op jit(solution)/shard_map/prep/pallas_call | solution.py:136
  25.0 5.2 %all-to-all-done.qg_ref = bf16[32,64,128]{2,1,0:T(8,128)(2,1)S(1)} async-done(((bf16[32,64,128]{2,1,0:T(8,128)(2,1)}), bf16[32,64,128]{2,1,0:T(8,128)(2,1)S(1)}, u32[]{:S(2)}, u32[]{:S(2)}) %all-to-all-start) | async-done | bytes 524320 | tf_op jit(solution)/shard_map/all_to_all | solution.py:318
  30.2 8.0 %attn.1 = bf16[32,72,128]{2,1,0:T(8,128)(2,1)S(1)} custom-call(s32[1]{0:T(128)S(6)} %copy.8.plen_ref, bf16[32,64,128]{2,1,0:T(8,128)(2,1)S(1)} %all-to-all-done.qg_ref, bf16[4,8,2048,128]{3,2,1,0:T(8,128)(2,1)} %get-tuple-element.7.kv_hbm, f32[480,64,128]{2,1,0:T(8,128)} %get-tuple-element.8.own_hbm), custom_call_target="tpu_custom_call" | custom-call | flops 2147483648 | bytes 12582912 | tf_op jit(solution)/shard_map/attn/pallas_call | solution.py:251
  38.2 22.6 %all_to_all.20.r_ref = bf16[32,72,128]{2,1,0:T(8,128)(2,1)S(1)} all-to-all(bf16[32,72,128]{2,1,0:T(8,128)(2,1)S(1)} %attn.1), channel_id=1, replica_groups=mesh['prefix'=32,'samples'=8] {'prefix'}, dimensions={0} | all-to-all | bytes 1179648 | tf_op jit(solution)/shard_map/all_to_all | solution.py:318
  60.9 0.5 combine.1
  61.5 10.2 %all_to_all.21 = bf16[8,32,256]{2,1,0:T(8,128)(2,1)S(1)} all-to-all(bf16[8,32,256]{2,1,0:T(8,128)(2,1)S(1)} %combine.1), channel_id=1, replica_groups=mesh['prefix'=32,'samples'=8] {'samples'}, dimensions={0} | all-to-all | bytes 262144 | tf_op jit(solution)/shard_map/all_to_all | solution.py:318
  71.7 0.0 copy-done
  71.7 0.3 fusion
  72.0 22.1 %all_to_all.22 = bf16[32,8,1024]{2,1,0:T(8,128)(2,1)S(1)} all-to-all(bf16[32,8,1024]{2,1,0:T(8,128)(2,1)S(1)} %fusion), channel_id=1, replica_groups=mesh['prefix'=32,'samples'=8] {'prefix'}, dimensions={0} | all-to-all | bytes 1048576 | tf_op jit(solution)/shard_map/all_to_all | solution.py:318
  94.0 0.7 reduce_sum.12
Async XLA Ops:
  0.0 71.7 %copy-start = (bf16[256,1024]{1,0:T(8,128)(2,1)S(1)}, bf16[256,1024]{1,0:T(8,128)(2,1)}, u32[]{:S(2)}) copy-start(bf16[256,1024]{1,0:T(8,128)(2,1)} %param.13) | copy-start | bytes 1572868
  0.0 0.8 copy-start.1
  1.7 28.6 %all-to-all-start = ((bf16[32,64,128]{2,1,0:T(8,128)(2,1)}), bf16[32,64,128]{2,1,0:T(8,128)(2,1)S(1)}, u32[]{:S(2)}, u32[]{:S(2)}) async-start(bf16[32,64,128]{2,1,0:T(8,128)(2,1)} %spread.1), calls=%async_computation | async-start | bytes 1048576 | tf_op jit(solution)/shard_map/all_to_all | solution.py:318

commit v5 on v4

--- a/solution.py
+++ b/solution.py
@@ -184,13 +184,19 @@
             m = jnp.max(m, axis=1, keepdims=True) * cs
             ms[j][1] = jnp.broadcast_to(m, (R, D)).astype(jnp.bfloat16).astype(jnp.float32)
     acc = {}
+    part = {}
     def weigh(j, c):
-        m = ms[j][1]
-        z = s_s[j % nbuf][:, c * tile:(c + 1) * tile]
-        p = jnp.exp2(z * cs - jnp.concatenate([m] * (tile // D), axis=1)).astype(jnp.bfloat16)
-        at = slice(c * tile, (c + 1) * tile)
+        half = R // 2
+        wide = 2 * tile
+        h, cc = c % 2, c // 2
+        m = ms[j][1][h * half:(h + 1) * half]
+        at = slice(cc * wide, (cc + 1) * wide)
+        z = s_s[j % nbuf][h * half:(h + 1) * half, at]
+        p = jnp.exp2(z * cs - jnp.concatenate([m] * (wide // D), axis=1)).astype(jnp.bfloat16)
         o = jnp.dot(p, jnp.concatenate([v_ref[j, at, :], one_s[at, :]], axis=1), preferred_element_type=jnp.float32)
-        acc[j] = o if c == 0 else acc[j] + o
+        part[(j, h)] = o if cc == 0 else part[(j, h)] + o
+        if (c + 1) * tile == T:
+            acc[j] = jnp.concatenate([part[(j, 0)], part[(j, 1)]], axis=0)
     def finish(j):
         o = acc[j][:, :D]
         tot = acc[j][:, D:]

time: 95.1 us -> 94.7 us (level)
  no operation moved by 1% of the time
where the time goes in v5:
time: 94.7 us; the launch traced here: 94.3 us
  blocking collectives  54.9 us (58%)
  Pallas kernels  19.7 us (21%)
  starting transfers between devices  11.4 us (12%)
  waiting for transfers between devices  5.21 us (6%)
  between operations  1.34 us (1%)
    all_to_all x3, blocking collectives, swap(): return lax.all_to_all(x, axis, split_axis=0, concat_axis=0, tiled=True)  54.9 us
    all_to_all x1, starting transfers between devices, swap(): return lax.all_to_all(x, axis, split_axis=0, concat_axis=0, tiled=True)  11.4 us
    pallas_call x1, Pallas kernels, prep(): pl.pallas_call(functools.partial(prep_kernel, tb=tb, sb=sb, cs=LOG2E / ma...  10.7 us
    pallas_call x1, Pallas kernels, attn(): pl.pallas_call(functools.partial(attn_kernel, cs=LOG2E / math.sqrt(D), ti...  7.59 us
    all_to_all x1, waiting for transfers between devices, swap(): return lax.all_to_all(x, axis, split_axis=0, concat_axis=0, tiled=True)  5.21 us
  transfers between devices with their start and end apart: 1, of which 1 were waited for; matrix products, arithmetic and copies ran while one was open for 0% of the time, Pallas kernels for 11%

profile of v5, /device:TPU:32, one launch (start us, length us, event | category | flops | bytes accessed | tf_op | source)
XLA Modules:
  0.0 94.3 jit_solution(3097627487019839372)
XLA Ops:
  0.0 0.0 copy-start
  0.0 0.0 copy-start.1
  0.0 0.8 copy-done.1
  0.8 0.9 spread.1
  1.7 11.4 %all-to-all-start = ((bf16[32,64,128]{2,1,0:T(8,128)(2,1)}), bf16[32,64,128]{2,1,0:T(8,128)(2,1)S(1)}, u32[]{:S(2)}, u32[]{:S(2)}) async-start(bf16[32,64,128]{2,1,0:T(8,128)(2,1)} %spread.1), calls=%async_computation | async-start | bytes 1048576 | tf_op jit(solution)/shard_map/all_to_all | solution.py:324
  14.3 10.7 %prep.1 = (bf16[4,8,2048,128]{3,2,1,0:T(8,128)(2,1)}, f32[480,64,128]{2,1,0:T(8,128)}) custom-call(s32[1]{0:T(128)S(6)} %copy.8.plen_ref, s32[1]{0:T(128)S(6)} %copy.9.len_ref, bf16[2,8,32]{2,1,0:T(8,128)(2,1)} %bitcast.9, bf16[2,16384,128]{2,1,0:T(8,128)(2,1)} %bitcast.7, bf16[1,8192]{1,0:T(2,128)(2,1)} %q_ref.3, bf16[1,2,512,1024]{3,2,1,0:T(8,128)(2,1)} %cache_hbm.1), custom_call_target="tpu_custom_call" | custom-call | flops 16777216 | bytes 20971520 | tf_op jit(solution)/shard_map/prep/pallas_call | solution.py:136
  25.0 5.2 %all-to-all-done.qg_ref = bf16[32,64,128]{2,1,0:T(8,128)(2,1)S(1)} async-done(((bf16[32,64,128]{2,1,0:T(8,128)(2,1)}), bf16[32,64,128]{2,1,0:T(8,128)(2,1)S(1)}, u32[]{:S(2)}, u32[]{:S(2)}) %all-to-all-start) | async-done | bytes 524320 | tf_op jit(solution)/shard_map/all_to_all | solution.py:324
  30.2 7.6 %attn.1 = bf16[32,72,128]{2,1,0:T(8,128)(2,1)S(1)} custom-call(s32[1]{0:T(128)S(6)} %copy.8.plen_ref, bf16[32,64,128]{2,1,0:T(8,128)(2,1)S(1)} %all-to-all-done.qg_ref, bf16[4,8,2048,128]{3,2,1,0:T(8,128)(2,1)} %get-tuple-element.7.kv_hbm, f32[480,64,128]{2,1,0:T(8,128)} %get-tuple-element.8.own_hbm), custom_call_target="tpu_custom_call" | custom-call | flops 2147483648 | bytes 12582912 | tf_op jit(solution)/shard_map/attn/pallas_call | solution.py:257
  37.8 22.6 %all_to_all.20.r_ref = bf16[32,72,128]{2,1,0:T(8,128)(2,1)S(1)} all-to-all(bf16[32,72,128]{2,1,0:T(8,128)(2,1)S(1)} %attn.1), channel_id=1, replica_groups=mesh['prefix'=32,'samples'=8] {'prefix'}, dimensions={0} | all-to-all | bytes 1179648 | tf_op jit(solution)/shard_map/all_to_all | solution.py:324
  60.5 0.5 combine.1
  61.0 10.2 %all_to_all.21 = bf16[8,32,256]{2,1,0:T(8,128)(2,1)S(1)} all-to-all(bf16[8,32,256]{2,1,0:T(8,128)(2,1)S(1)} %combine.1), channel_id=1, replica_groups=mesh['prefix'=32,'samples'=8] {'samples'}, dimensions={0} | all-to-all | bytes 262144 | tf_op jit(solution)/shard_map/all_to_all | solution.py:324
  71.3 0.0 copy-done
  71.3 0.3 fusion
  71.6 22.1 %all_to_all.22 = bf16[32,8,1024]{2,1,0:T(8,128)(2,1)S(1)} all-to-all(bf16[32,8,1024]{2,1,0:T(8,128)(2,1)S(1)} %fusion), channel_id=1, replica_groups=mesh['prefix'=32,'samples'=8] {'prefix'}, dimensions={0} | all-to-all | bytes 1048576 | tf_op jit(solution)/shard_map/all_to_all | solution.py:324
  93.6 0.7 reduce_sum.12
Async XLA Ops:
  0.0 71.3 %copy-start = (bf16[256,1024]{1,0:T(8,128)(2,1)S(1)}, bf16[256,1024]{1,0:T(8,128)(2,1)}, u32[]{:S(2)}) copy-start(bf16[256,1024]{1,0:T(8,128)(2,1)} %param.13) | copy-start | bytes 1572868
  0.0 0.8 copy-start.1
  1.7 28.6 %all-to-all-start = ((bf16[32,64,128]{2,1,0:T(8,128)(2,1)}), bf16[32,64,128]{2,1,0:T(8,128)(2,1)S(1)}, u32[]{:S(2)}, u32[]{:S(2)}) async-start(bf16[32,64,128]{2,1,0:T(8,128)(2,1)} %spread.1), calls=%async_computation | async-start | bytes 1048576 | tf_op jit(solution)/shard_map/all_to_all | solution.py:324

commit v6 on v5

--- a/solution.py
+++ b/solution.py
@@ -298,19 +298,31 @@
         name="combine",
     )(r)
 
-def spread_kernel(q_ref, o_ref):
-    M, HQ, D = o_ref.shape
+def spread_kernel(q_hbm, o_hbm, q_ref, x_ref, q_sem, o_sem):
+    M, HQ, D = o_hbm.shape
+    load = pltpu.make_async_copy(q_hbm, q_ref, q_sem)
+    load.start()
+    load.wait()
     q = q_ref[...].astype(jnp.float32)
     x = jnp.concatenate([q[:, h * D:(h + 1) * D] for h in range(HQ)], axis=0).astype(jnp.bfloat16)
-    for i in range(M):
-        o_ref[i] = x
+    part = x_ref.shape[0]
+    for i in range(part):
+        x_ref[i] = x
+    copies = [pltpu.make_async_copy(x_ref, o_hbm.at[i * part:(i + 1) * part], o_sem.at[i]) for i in range(M // part)]
+    for copy in copies:
+        copy.start()
+    for copy in copies:
+        copy.wait()
 
 def spread(q, members, width):
-    vm = pl.BlockSpec(memory_space=pltpu.VMEM)
+    hbm = pl.BlockSpec(memory_space=pltpu.HBM)
+    rows = q.shape[1] // width
     return pl.pallas_call(
-        spread_kernel, in_specs=[vm], out_specs=vm,
-        out_shape=jax.ShapeDtypeStruct((members, q.shape[1] // width, width), q.dtype),
-        compiler_params=pltpu.CompilerParams(vmem_limit_bytes=10 << 20),
+        spread_kernel, in_specs=[hbm], out_specs=hbm,
+        out_shape=jax.ShapeDtypeStruct((members, rows, width), q.dtype),
+        scratch_shapes=[pltpu.VMEM(q.shape, q.dtype), pltpu.VMEM((8, rows, width), q.dtype),
+                        pltpu.SemaphoreType.DMA, pltpu.SemaphoreType.DMA((members // 8,))],
+        compiler_params=pltpu.CompilerParams(vmem_limit_bytes=63_480_000),
         cost_estimate=pl.CostEstimate(flops=1 << 18, bytes_accessed=1 << 19, transcendentals=0),
         name="spread",
     )(q)

time: 94.7 us -> 94.7 us (level)
  no operation moved by 1% of the time
where the time goes in v6:
time: 94.7 us; the launch traced here: 94.3 us
  blocking collectives  54.9 us (58%)
  Pallas kernels  20.5 us (22%)
  starting transfers between devices  11.4 us (12%)
  waiting for transfers between devices  5.23 us (6%)
  between operations  1.35 us (1%)
    all_to_all x3, blocking collectives, swap(): return lax.all_to_all(x, axis, split_axis=0, concat_axis=0, tiled=True)  54.9 us
    all_to_all x1, starting transfers between devices, swap(): return lax.all_to_all(x, axis, split_axis=0, concat_axis=0, tiled=True)  11.4 us
    pallas_call x1, Pallas kernels, prep(): pl.pallas_call(functools.partial(prep_kernel, tb=tb, sb=sb, cs=LOG2E / ma...  10.7 us
    pallas_call x1, Pallas kernels, attn(): pl.pallas_call(functools.partial(attn_kernel, cs=LOG2E / math.sqrt(D), ti...  7.59 us
    all_to_all x1, waiting for transfers between devices, swap(): return lax.all_to_all(x, axis, split_axis=0, concat_axis=0, tiled=True)  5.23 us
  transfers between devices with their start and end apart: 1, of which 1 were waited for; matrix products, arithmetic and copies ran while one was open for 0% of the time, Pallas kernels for 11%

profile of v6, /device:TPU:32, one launch (start us, length us, event | category | flops | bytes accessed | tf_op | source)
XLA Modules:
  0.0 94.3 jit_solution(7546095661427797605)
XLA Ops:
  0.0 0.0 copy-start
  0.0 1.7 %spread.1 = bf16[32,64,128]{2,1,0:T(8,128)(2,1)} custom-call(bf16[1,8192]{1,0:T(2,128)(2,1)} %q_ref.1), custom_call_target="tpu_custom_call" | custom-call | flops 262144 | bytes 524288 | tf_op jit(solution)/shard_map/spread/pallas_call | solution.py:320
  1.7 11.4 %all-to-all-start = ((bf16[32,64,128]{2,1,0:T(8,128)(2,1)}), bf16[32,64,128]{2,1,0:T(8,128)(2,1)S(1)}, u32[]{:S(2)}, u32[]{:S(2)}) async-start(bf16[32,64,128]{2,1,0:T(8,128)(2,1)} %spread.1), calls=%async_computation | async-start | bytes 1048576 | tf_op jit(solution)/shard_map/all_to_all | solution.py:336
  14.4 10.7 %prep.1 = (bf16[4,8,2048,128]{3,2,1,0:T(8,128)(2,1)}, f32[480,64,128]{2,1,0:T(8,128)}) custom-call(s32[1]{0:T(128)S(6)} %copy.8.plen_ref, s32[1]{0:T(128)S(6)} %copy.9.len_ref, bf16[2,8,32]{2,1,0:T(8,128)(2,1)} %bitcast.9, bf16[2,16384,128]{2,1,0:T(8,128)(2,1)} %bitcast.7, bf16[1,8192]{1,0:T(2,128)(2,1)} %q_ref.1, bf16[1,2,512,1024]{3,2,1,0:T(8,128)(2,1)} %cache_hbm.1), custom_call_target="tpu_custom_call" | custom-call | flops 16777216 | bytes 20971520 | tf_op jit(solution)/shard_map/prep/pallas_call | solution.py:136
  25.0 5.2 %all-to-all-done.qg_ref = bf16[32,64,128]{2,1,0:T(8,128)(2,1)S(1)} async-done(((bf16[32,64,128]{2,1,0:T(8,128)(2,1)}), bf16[32,64,128]{2,1,0:T(8,128)(2,1)S(1)}, u32[]{:S(2)}, u32[]{:S(2)}) %all-to-all-start) | async-done | bytes 524320 | tf_op jit(solution)/shard_map/all_to_all | solution.py:336
  30.3 7.6 %attn.1 = bf16[32,72,128]{2,1,0:T(8,128)(2,1)S(1)} custom-call(s32[1]{0:T(128)S(6)} %copy.8.plen_ref, bf16[32,64,128]{2,1,0:T(8,128)(2,1)S(1)} %all-to-all-done.qg_ref, bf16[4,8,2048,128]{3,2,1,0:T(8,128)(2,1)} %get-tuple-element.7.kv_hbm, f32[480,64,128]{2,1,0:T(8,128)} %get-tuple-element.8.own_hbm), custom_call_target="tpu_custom_call" | custom-call | flops 2147483648 | bytes 12582912 | tf_op jit(solution)/shard_map/attn/pallas_call | solution.py:257
  37.9 22.6 %all_to_all.20.r_ref = bf16[32,72,128]{2,1,0:T(8,128)(2,1)S(1)} all-to-all(bf16[32,72,128]{2,1,0:T(8,128)(2,1)S(1)} %attn.1), channel_id=1, replica_groups=mesh['prefix'=32,'samples'=8] {'prefix'}, dimensions={0} | all-to-all | bytes 1179648 | tf_op jit(solution)/shard_map/all_to_all | solution.py:336
  60.5 0.5 combine.1
  61.0 10.2 %all_to_all.21 = bf16[8,32,256]{2,1,0:T(8,128)(2,1)S(1)} all-to-all(bf16[8,32,256]{2,1,0:T(8,128)(2,1)S(1)} %combine.1), channel_id=1, replica_groups=mesh['prefix'=32,'samples'=8] {'samples'}, dimensions={0} | all-to-all | bytes 262144 | tf_op jit(solution)/shard_map/all_to_all | solution.py:336
  71.3 0.0 copy-done
  71.3 0.3 fusion
  71.6 22.1 %all_to_all.22 = bf16[32,8,1024]{2,1,0:T(8,128)(2,1)S(1)} all-to-all(bf16[32,8,1024]{2,1,0:T(8,128)(2,1)S(1)} %fusion), channel_id=1, replica_groups=mesh['prefix'=32,'samples'=8] {'prefix'}, dimensions={0} | all-to-all | bytes 1048576 | tf_op jit(solution)/shard_map/all_to_all | solution.py:336
  93.7 0.7 reduce_sum.12
Async XLA Ops:
  0.0 71.3 %copy-start = (bf16[256,1024]{1,0:T(8,128)(2,1)S(1)}, bf16[256,1024]{1,0:T(8,128)(2,1)}, u32[]{:S(2)}) copy-start(bf16[256,1024]{1,0:T(8,128)(2,1)} %param.13) | copy-start | bytes 1572868
  1.7 28.6 %all-to-all-start = ((bf16[32,64,128]{2,1,0:T(8,128)(2,1)}), bf16[32,64,128]{2,1,0:T(8,128)(2,1)S(1)}, u32[]{:S(2)}, u32[]{:S(2)}) async-start(bf16[32,64,128]{2,1,0:T(8,128)(2,1)} %spread.1), calls=%async_computation | async-start | bytes 1048576 | tf_op jit(solution)/shard_map/all_to_all | solution.py:336
